TPU v7x, 512 devices: a whole 4x4x16 slice. The times are simulated.
512 devices in a mesh: band: 128 (over z, y, core), mode: 4 (over x).
Axes of the slice: x: 4, y: 4, z: 16, core: 2. Of those that a mesh axis runs over, the one named last changes fastest.
Arguments:
- velocity: bfloat16 [1, 131072, 1024], P(None, ('band', 'mode')), may hold values from -6 to 6
- radiation_modes: bfloat16 [131072, 1024], P('band', 'mode'), may hold values from -0.03125 to 0.03125
- resistance: float32 [128, 1024, 1024], P('band', None, 'mode'), as said below
- mode_ranks: int32 [128], P('band'), may hold values from 128 to 1024, as said below
- freq_table: int32 [512], replicated, may hold values from 0 to 511, each once
Outputs:
- adjoint_force: bfloat16 [1, 131072, 1024], P(None, ('band', 'mode'))
Inputs may be any that keep to these rules, and one draw needn't show every extreme that they name: `resistance`: each band's matrix is symmetric. `mode_ranks`: the ranks never fall with the band index; the first band keeps 1024 // 8 modes and the last 1024.
All inputs are finite; a program needn't handle non-finite values.
Results may differ from a plain program's by a relative error of at most 0.015.
Values may be sent and summed in bfloat16 or wider, within the bound.
No kernel may reach another device: no remote copies, remote signals or barrier semaphores. Data moves between devices by JAX's collectives and lax.ppermute only.
A program may use at most 64 MiB of HBM per device.

v0:
```python
import math

import jax
import jax.numpy as jnp
from jax import lax
from jax.sharding import Mesh
from jax.sharding import PartitionSpec as P

BAND = ("band_0", "band_1", "band_2")
BAND_MODE = ("band_0", "band_1", "band_2", "mode")


def in_order(parts, dim):
    parts = jnp.moveaxis(parts, 0, dim)
    shape = parts.shape
    return parts.reshape(*shape[:dim], shape[dim] * shape[dim + 1], *shape[dim + 2 :])


def sent_to_all(value, axis):
    copies = jnp.broadcast_to(value, (lax.axis_size(axis), *value.shape))
    return lax.all_to_all(copies, axis, split_axis=0, concat_axis=0, tiled=True)


def collect(value, axis, dim):
    return in_order(sent_to_all(value, axis), dim)


def gather_in_order(value, axes, sequence):
    parts = value
    for k in sequence:
        parts = lax.all_gather(parts, axes[k])
    done = sequence[::-1]
    back = [done.index(k) for k in range(len(axes))]
    parts = parts.transpose(*back, *range(len(axes), parts.ndim))
    return parts.reshape(-1, *value.shape)


def gathered_by_axis(value, axes, sequence, dim):
    return in_order(gather_in_order(value, axes, sequence), dim)


def make_table(freq_table, step_count):
    times = jnp.arange(step_count, dtype=jnp.int32)
    phases = times[:, None] * freq_table[None, :] % step_count
    angles = phases.astype(jnp.float32) * (2.0 * math.pi / step_count)
    norming = 1.0 / math.sqrt(step_count)
    table = jnp.stack([jnp.cos(angles), -jnp.sin(angles)], axis=1) * norming
    return table.astype(jnp.bfloat16)


def add_sources(received):
    return jnp.sum(received, axis=0)


def per_device(velocity, radiation_modes, resistance, mode_ranks, freq_table):
    windows = velocity.shape[0]
    step_count = velocity.shape[2]
    mode_cols = radiation_modes.shape[1]
    dft_table = make_table(freq_table, step_count)
    spectra = jnp.einsum(
        "wpt,tcf->wpcf", velocity, dft_table, preferred_element_type=jnp.float32
    ).astype(jnp.bfloat16)
    partial_value = jnp.einsum(
        "wpcf,pr->wrcf",
        collect(spectra, "mode", 1),
        radiation_modes,
        preferred_element_type=jnp.float32,
    )
    coefficients = add_sources(
        lax.all_to_all(
            partial_value[None].astype(jnp.bfloat16), BAND, split_axis=4, concat_axis=0, tiled=True
        ).astype(jnp.float32)
    )
    offset = lax.axis_index("mode") * mode_cols
    rank_here = mode_ranks[0]
    kept_mask = (offset + jnp.arange(mode_cols, dtype=jnp.int32) < rank_here).astype(jnp.float32)
    kept_mask = kept_mask[None, :, None, None]
    coefficients = coefficients * kept_mask
    matrix = resistance[0]
    gathered = collect(coefficients, "mode", 1)
    forcing = jnp.einsum("ji,wjcf->wicf", matrix, gathered)
    forcing = (2.0 * forcing * kept_mask).astype(jnp.bfloat16)
    pieces = gathered_by_axis(forcing[None], BAND_MODE, (0, 1, 3, 2), 0)
    band_count = lax.axis_size(BAND)
    mode_count = lax.axis_size("mode")
    slots_here = forcing.shape[3]
    pieces = pieces.reshape(band_count, mode_count, windows, mode_cols, 2, slots_here)
    collected = pieces.transpose(2, 1, 3, 4, 0, 5).reshape(
        windows, mode_count * mode_cols, 2, band_count * slots_here
    )
    own_basis = lax.all_to_all(radiation_modes, "mode", split_axis=0, concat_axis=1, tiled=True)
    surface_force = jnp.einsum(
        "pr,wrcf->wpcf", own_basis, collected, preferred_element_type=jnp.float32
    ).astype(jnp.bfloat16)
    history = jnp.einsum(
        "wpcf,tcf->wpt", surface_force, dft_table, preferred_element_type=jnp.float32
    )
    return history.astype(jnp.bfloat16)


def solution(mesh):
    torus = Mesh(
        mesh.devices.reshape(16, 4, 2, mesh.shape["mode"]), ("band_0", "band_1", "band_2", "mode")
    )
    in_specs = (P(None, BAND_MODE, None), P(BAND, "mode"), P(BAND, None, "mode"), P(BAND), P())
    out_specs = P(None, BAND_MODE, None)
    return jax.shard_map(
        per_device, mesh=torus, in_specs=in_specs, out_specs=out_specs, check_vma=False
    )
```

profile of v0, /device:TPU:1, one launch (start us, length us, event | category | flops | bytes accessed | tf_op | source)
XLA Modules:
  0.0 227.9 jit_solution(18398536308180994929)
XLA Ops:
  6.5 9.1 %fusion.16 = (f32[1024,1,512]{0,2,1:T(8,128)S(1)}, f32[1024,1,512]{0,2,1:T(8,128)S(1)}) fusion(s32[512]{0:T(512)} %param.9), kind=kLoop, calls=%fused_computation.27 | loop fusion | flops 7864320 | bytes 4196352 | tf_op jit(solution)/shard_map/cos | solution.py:47
  15.7 1.3 copy-done.1
  17.0 0.6 copy-done.2
  17.6 0.7 fusion.8
  18.5 26.3 %all_to_all.38 = bf16[4,1,256,2,512]{2,4,3,1,0:T(8,128)(2,1)S(1)} all-to-all(bf16[4,1,256,2,512]{2,4,3,1,0:T(8,128)(2,1)S(1)} %broadcast_in_dim.4), channel_id=1, replica_groups=mesh['band_0'=16,'band_1'=4,'band_2'=2,'mode'=4] {'mode'}, dimensions={0} | all-to-all | bytes 4194304 | tf_op jit(solution)/shard_map/all_to_all | solution.py:21
  44.8 1.6 copy.29
  46.5 2.7 %reshape.159 = bf16[1024,2,512]{0,2,1:T(8,128)(2,1)} reshape(bf16[4,1,256,2,512]{2,0,4,3,1:T(4,128)(2,1)S(1)} %copy.29) | data formatting | bytes 4194304 | tf_op jit(solution)/shard_map/reshape.4
  49.2 2.4 %fusion.9 = bf16[1,1,256,2,512]{2,4,3,1,0:T(8,128)(2,1)S(1)} fusion(bf16[1024,2,512]{0,2,1:T(8,128)(2,1)} %reshape.159, bf16[1024,256]{1,0:T(8,128)(2,1)} %param.6), kind=kOutput, calls=%fused_computation.18 | convolution fusion | flops 537133056 | bytes 3145728 | tf_op jit(solution)/shard_map/wpcf,pr->wrcf/dot_general | solution.py:63
  51.6 1.3 copy.30
  52.9 24.7 %all-to-all-start.1 = ((bf16[1,1,256,2,512]{2,3,1,0,4:T(2,128)(2,1)}), bf16[1,1,256,2,512]{2,3,1,0,4:T(2,128)(2,1)S(1)}, u32[]{:S(2)}, u32[]{:S(2)}) async-start(bf16[1,1,256,2,512]{2,3,1,0,4:T(2,128)(2,1)} %copy.30), calls=%async_computation.1 | async-start | bytes 1048576 | tf_op jit(solution)/shard_map/all_to_all | solution.py:70
  78.3 30.1 %all-to-all-done.1 = bf16[1,1,256,2,512]{2,3,1,0,4:T(2,128)(2,1)S(1)} async-done(((bf16[1,1,256,2,512]{2,3,1,0,4:T(2,128)(2,1)}), bf16[1,1,256,2,512]{2,3,1,0,4:T(2,128)(2,1)S(1)}, u32[]{:S(2)}, u32[]{:S(2)}) %all-to-all-start.1) | async-done | bytes 524320 | tf_op jit(solution)/shard_map/all_to_all | solution.py:70
  108.9 0.6 broadcast_in_dim.10
  109.5 3.3 %all-to-all-start.2 = ((bf16[4,1,256,2,4]{2,4,3,1,0:T(4,128)(2,1)}), bf16[4,1,256,2,4]{2,4,3,1,0:T(4,128)(2,1)S(1)}, u32[]{:S(2)}, u32[]{:S(2)}) async-start(bf16[4,1,256,2,4]{2,4,3,1,0:T(4,128)(2,1)} %broadcast_in_dim.10), calls=%async_computation.2 | async-start | bytes 32768 | tf_op jit(solution)/shard_map/all_to_all | solution.py:21
  112.8 4.1 %all-to-all-done.2 = bf16[4,1,256,2,4]{2,4,3,1,0:T(4,128)(2,1)S(1)} async-done(((bf16[4,1,256,2,4]{2,4,3,1,0:T(4,128)(2,1)}), bf16[4,1,256,2,4]{2,4,3,1,0:T(4,128)(2,1)S(1)}, u32[]{:S(2)}, u32[]{:S(2)}) %all-to-all-start.2) | async-done | bytes 16416 | tf_op jit(solution)/shard_map/all_to_all | solution.py:21
  117.2 23.4 %all-gather = bf16[16,256,2,4]{1,3,2,0:T(4,128)(2,1)S(1)} all-gather(bf16[1,256,2,4]{1,3,2,0:T(4,128)(2,1)S(1)} %fusion.14), channel_id=2, replica_groups=mesh['band_0'=16,'band_1'=4,'band_2'=2,'mode'=4] {'band_0'}, dimensions={0}, use_global_device_ids=true | all-gather | bytes 69632 | tf_op jit(solution)/shard_map/all_gather | solution.py:31
  140.6 9.7 %all-gather.1 = bf16[64,256,2,4]{1,3,2,0:T(4,128)(2,1)S(1)} all-gather(bf16[16,256,2,4]{1,3,2,0:T(4,128)(2,1)S(1)} %all-gather), channel_id=3, replica_groups=mesh['band_0'=16,'band_1'=4,'band_2'=2,'mode'=4] {'band_1'}, dimensions={0}, use_global_device_ids=true | all-gather | bytes 327680 | tf_op jit(solution)/shard_map/all_gather | solution.py:31
  150.3 0.8 copy.33
  151.1 32.0 %all-gather.7.cloned.1.call-done = bf16[16,16,1,1,256,2,4]{4,1,6,5,3,2,0:T(8,128)(2,1)} async-done(((bf16[4,16,1,1,256,2,4]{4,1,6,5,3,2,0:T(8,128)(2,1)}), bf16[16,16,1,1,256,2,4]{4,1,6,5,3,2,0:T(8,128)(2,1)}) %all-gather.7.cloned.1.call-update) | async-done | bytes 1048592 | tf_op jit(solution)/shard_map/all_gather | solution.py:31
  183.2 10.6 %all_to_all.39 = bf16[4,256,256]{2,1,0:T(8,128)(2,1)S(1)} all-to-all(bf16[4,256,256]{2,1,0:T(8,128)(2,1)S(1)} %bitcast.85), channel_id=1, replica_groups=mesh['band_0'=16,'band_1'=4,'band_2'=2,'mode'=4] {'mode'}, dimensions={0} | all-to-all | bytes 1048576 | tf_op jit(solution)/shard_map/all_to_all | solution.py:91
  194.2 1.2 reshape.171
  195.4 13.7 %all-gather.9.cloned.1.call-done = bf16[8,4,16,1,1,256,2,4]{5,2,7,6,4,3,1,0:T(8,128)(2,1)} async-done(((bf16[4,4,16,1,1,256,2,4]{5,2,7,6,4,3,1,0:T(8,128)(2,1)}), bf16[8,4,16,1,1,256,2,4]{5,2,7,6,4,3,1,0:T(8,128)(2,1)}) %all-gather.9.cloned.1.call-update) | async-done | bytes 2097168 | tf_op jit(solution)/shard_map/all_gather | solution.py:31
  209.0 3.2 %copy.35 = bf16[16,4,2,4,1,1,256,2,4]{6,3,8,2,1,0,7,5,4:T(4,128)(2,1)S(1)} copy(bf16[16,4,2,4,1,1,256,2,4]{6,0,8,7,1,3,2,5,4:T(8,128)(2,1)} %bitcast.80) | data formatting | bytes 4194304 | tf_op jit(solution)/shard_map/transpose | solution.py:34
  212.3 2.7 %reshape.161 = bf16[1024,2,512]{0,2,1:T(8,128)(2,1)} reshape(bf16[1,4,256,2,128,4]{2,1,5,4,3,0:T(4,128)(2,1)S(1)} %bitcast.79) | data formatting | bytes 4194304 | tf_op jit(solution)/shard_map/reshape.11
  215.0 6.1 %fusion.11 = bf16[1,256,1024]{2,1,0:T(8,128)(2,1)} fusion(bf16[1024,2,512]{0,2,1:T(8,128)(2,1)} %reshape.161, bf16[256,1024,1]{1,0,2:T(8,128)(2,1)} %reshape.171, f32[1024,1,512]{0,2,1:T(8,128)} %copy-done.2, f32[1024,1,512]{0,2,1:T(8,128)} %copy-done.1), kind=kOutput, calls=%fused_computation.20 | convolution fusion | flops 1077411840 | bytes 7340032 | tf_op jit(solution)/shard_map/wpcf,tcf->wpt/dot_general | solution.py:95
  (21 shorter events, 1.4 us)
Async XLA Ops:
  6.5 110.4 %copy-start = (f32[1,1024,256]{2,1,0:T(8,128)S(1)}, f32[1,1024,256]{2,1,0:T(8,128)}, u32[]{:S(2)}) copy-start(f32[1,1024,256]{2,1,0:T(8,128)} %param.7) | copy-start | bytes 3145732
  6.5 11.1 %copy-start.4 = (bf16[1,256,1024]{2,1,0:T(8,128)(2,1)S(1)}, bf16[1,256,1024]{2,1,0:T(8,128)(2,1)}, u32[]{:S(2)}) copy-start(bf16[1,256,1024]{2,1,0:T(8,128)(2,1)} %param.5) | copy-start | bytes 1572868
  15.7 1.3 copy-start.1
  15.7 1.9 copy-start.2
  52.9 55.5 %all-to-all-start.1 = ((bf16[1,1,256,2,512]{2,3,1,0,4:T(2,128)(2,1)}), bf16[1,1,256,2,512]{2,3,1,0,4:T(2,128)(2,1)S(1)}, u32[]{:S(2)}, u32[]{:S(2)}) async-start(bf16[1,1,256,2,512]{2,3,1,0,4:T(2,128)(2,1)} %copy.30), calls=%async_computation.1 | async-start | bytes 1048576 | tf_op jit(solution)/shard_map/all_to_all | solution.py:70
  77.6 105.6 %copy-start.3 = (bf16[1024,256]{1,0:T(8,128)(2,1)S(1)}, bf16[1024,256]{1,0:T(8,128)(2,1)}, u32[]{:S(2)}) copy-start(bf16[1024,256]{1,0:T(8,128)(2,1)} %param.6) | copy-start | bytes 1572868
  109.5 7.4 %all-to-all-start.2 = ((bf16[4,1,256,2,4]{2,4,3,1,0:T(4,128)(2,1)}), bf16[4,1,256,2,4]{2,4,3,1,0:T(4,128)(2,1)S(1)}, u32[]{:S(2)}, u32[]{:S(2)}) async-start(bf16[4,1,256,2,4]{2,4,3,1,0:T(4,128)(2,1)} %broadcast_in_dim.10), calls=%async_computation.2 | async-start | bytes 32768 | tf_op jit(solution)/shard_map/all_to_all | solution.py:21
  112.8 70.3 %all-gather.7.cloned.1.call-start = ((), (), s32[]{:S(2)}) async-start(), calls=%async_computation.4 | async-start | bytes 1310720 | tf_op jit(solution)/shard_map/all_gather | solution.py:31
  151.0 58.0 %all-gather.9.cloned.1.call-start = ((), (), s32[]{:S(2)}) async-start(), calls=%async_computation.5 | async-start | bytes 3145728 | tf_op jit(solution)/shard_map/all_gather | solution.py:31
Sparse Core Ops, SparseCore 0:
  151.2 31.9 all-gather.6
  185.2 23.7 all-gather.8
where the time goes:
time: 228 us
  waiting for transfers between devices  79.9 us (35%)
  blocking collectives  70 us (31%)
  starting transfers between devices  28 us (12%)
  local copies, waits for them, and re-layouts  16.6 us (7%)
  between operations  14.2 us (6%)
  other arithmetic  9.64 us (4%)
  matrix products  9.44 us (4%)
    all_gather x2, waiting for transfers between devices, gather_in_order(): parts = lax.all_gather(parts, axes[k])  45.7 us
    all_gather x2, blocking collectives, gather_in_order(): parts = lax.all_gather(parts, axes[k])  33.1 us
    all_to_all x1, waiting for transfers between devices, per_device(): lax.all_to_all(partial_value[None].astype(jnp.bfloat16), BAND, split_axis...  30.1 us
    all_to_all x1, blocking collectives, sent_to_all(): return lax.all_to_all(copies, axis, split_axis=0, concat_axis=0, tiled=True)  26.3 us
    all_to_all x1, starting transfers between devices, per_device(): lax.all_to_all(partial_value[None].astype(jnp.bfloat16), BAND, split_axis...  24.7 us
    all_to_all x1, blocking collectives, per_device(): lax.all_to_all(radiation_modes, 'mode', split_axis=0, concat_axis=1, tile...  10.6 us
    cos x1, other arithmetic, make_table(): table = jnp.stack([jnp.cos(angles), -jnp.sin(angles)], axis=1) * norming  9.14 us
    dot_general x1, matrix products, per_device(): jnp.einsum('wpcf,tcf->wpt', surface_force, dft_table, preferred_element_t...  6.13 us
  transfers between devices with their start and end apart: 4, of which 4 were waited for; matrix products, arithmetic and copies ran while one was open for 1% of the time, Pallas kernels for 0%

commit v1 on v0

v1 whole, which is shorter than its diff:
```python
import functools
import math

import jax
import jax.numpy as jnp
from jax import lax
from jax.experimental import pallas as pl
from jax.experimental.pallas import tpu as pltpu
from jax.sharding import Mesh
from jax.sharding import PartitionSpec as P

Z, Y, CORE, MODE = "band_0", "band_1", "band_2", "mode"
F32, BF16 = jnp.float32, jnp.bfloat16
LANES = 128
VMEM = 24 * 1024 * 1024


def call(kernel, out_shape, flops, **options):
    whole = pl.BlockSpec(memory_space=pltpu.VMEM)
    return pl.pallas_call(
        kernel,
        out_shape=out_shape,
        compiler_params=pltpu.CompilerParams(vmem_limit_bytes=VMEM),
        cost_estimate=pl.CostEstimate(flops=flops, bytes_accessed=4 << 20, transcendentals=0),
        **options,
    )


def dot(a, b):
    return jnp.dot(a, b, preferred_element_type=F32)


def dot_t(a, b):
    return lax.dot_general(a, b, (((1,), (1,)), ((), ())), preferred_element_type=F32)


def spectra_kernel(steps, freq_ref, part_ref, velocity_ref, table_ref, spectra_ref):
    rows = freq_ref.shape[0]
    freq = freq_ref[...]
    part = part_ref[...]
    low = lax.broadcasted_iota(jnp.int32, (rows, LANES), 1)
    turn = 2.0 * math.pi / steps
    phase = (low * freq + part * (steps // 4)) & (steps - 1)
    angle = phase.astype(F32) * turn
    cos_low = jnp.cos(angle) * (1.0 / math.sqrt(steps))
    sin_low = jnp.sin(angle) * (1.0 / math.sqrt(steps))
    for high in range(steps // LANES):
        coarse = ((high * LANES * freq) & (steps - 1)).astype(F32) * turn
        piece = cos_low * jnp.cos(coarse) - sin_low * jnp.sin(coarse)
        table_ref[:, high * LANES : (high + 1) * LANES] = piece.astype(BF16)
    spectra_ref[...] = dot_t(table_ref[...], velocity_ref[...]).astype(BF16)


def make_spectra(freq, part, velocity):
    rows = freq.shape[0]
    patches, steps = velocity.shape
    tile = rows // 4
    return call(
        functools.partial(spectra_kernel, steps),
        (
            jax.ShapeDtypeStruct((rows, steps), BF16),
            jax.ShapeDtypeStruct((rows, patches), BF16),
        ),
        2 * rows * patches * steps,
        grid=(4,),
        in_specs=[
            pl.BlockSpec((tile, 1), lambda i: (i, 0)),
            pl.BlockSpec((tile, 1), lambda i: (i, 0)),
            pl.BlockSpec((patches, steps), lambda i: (0, 0)),
        ],
        out_specs=(
            pl.BlockSpec((tile, steps), lambda i: (i, 0)),
            pl.BlockSpec((tile, patches), lambda i: (i, 0)),
        ),
    )(freq, part, velocity)


def partial_kernel(spectra_ref, basis_ref, out_ref):
    width = basis_ref.shape[2]
    for k in range(basis_ref.shape[0]):
        out_ref[:, k * width : (k + 1) * width] = dot(spectra_ref[...], basis_ref[k]).astype(BF16)


def make_partial(spectra, basis, half):
    rows, patches = spectra.shape
    parts, _, width = basis.shape
    tile = rows // 4
    return call(
        partial_kernel,
        jax.ShapeDtypeStruct((rows // 2, parts * width), BF16),
        rows * patches * parts * width,
        grid=(2,),
        in_specs=[
            pl.BlockSpec((tile, patches), lambda i: (2 * half + i, 0)),
            pl.BlockSpec(basis.shape, lambda i: (0, 0, 0)),
        ],
        out_specs=pl.BlockSpec((tile, parts * width), lambda i: (i, 0)),
    )(spectra, basis)


def forcing_kernel(rank_ref, offset_ref, coef_ref, matrix_ref, out_ref):
    rank = rank_ref[0]
    total = coef_ref[0].astype(F32)
    for k in range(1, coef_ref.shape[0]):
        total = total + coef_ref[k].astype(F32)
    index = lax.broadcasted_iota(jnp.int32, total.shape, 1)
    total = jnp.where(index < rank, total, 0.0)
    forcing = dot(total.astype(BF16), matrix_ref[...].astype(BF16))
    index = lax.broadcasted_iota(jnp.int32, forcing.shape, 1) + offset_ref[0]
    out_ref[...] = jnp.where(index < rank, 2.0 * forcing, 0.0).astype(BF16)


def make_forcing(rank, offset, coef, matrix):
    rows = coef.shape[1]
    smem = pl.BlockSpec(memory_space=pltpu.SMEM)
    vmem = pl.BlockSpec(memory_space=pltpu.VMEM)
    return call(
        forcing_kernel,
        jax.ShapeDtypeStruct((rows, matrix.shape[1]), BF16),
        2 * rows * matrix.shape[0] * matrix.shape[1],
        in_specs=[smem, smem, vmem, vmem],
        out_specs=vmem,
    )(rank, offset, coef, matrix)


def history_kernel(basis_ref, forcing_ref, table_ref, *rest):
    out_ref = rest[-1]
    total = dot_t(basis_ref[0], forcing_ref[0])
    for k in range(1, basis_ref.shape[0]):
        total = total + dot_t(basis_ref[k], forcing_ref[k])
    history = dot(total.astype(BF16), table_ref[...])
    if len(rest) > 1:
        history = history + rest[0][...]
    out_ref[...] = history.astype(out_ref.dtype)


def make_history(basis, forcing, table, half, before, dtype):
    parts, patches, width = basis.shape
    rows = forcing.shape[1]
    steps = table.shape[1]
    more = [] if before is None else [before]
    whole = pl.BlockSpec(memory_space=pltpu.VMEM)
    return call(
        history_kernel,
        jax.ShapeDtypeStruct((patches, steps), dtype),
        2 * rows * patches * (steps + parts * width),
        grid=(1,),
        in_specs=[
            pl.BlockSpec(basis.shape, lambda i: (0, 0, 0)),
            pl.BlockSpec(forcing.shape, lambda i: (0, 0, 0)),
            pl.BlockSpec((rows, steps), lambda i: (half, 0)),
        ]
        + [pl.BlockSpec(x.shape, lambda i: (0, 0)) for x in more],
        out_specs=pl.BlockSpec((patches, steps), lambda i: (0, 0)),
    )(basis, forcing, table, *more)


def exchange(value, axis):
    return lax.all_to_all(value, axis, split_axis=0, concat_axis=0, tiled=True)


def spread(value, axis):
    return exchange(jnp.broadcast_to(value, (lax.axis_size(axis), *value.shape)), axis)


def reduced(value, axis):
    count = lax.axis_size(axis)
    parts = exchange(value.reshape(count, value.shape[0] // count, value.shape[1]), axis)
    return jnp.sum(parts.astype(F32), axis=0).astype(BF16)


def swap_cores(value):
    return lax.ppermute(value, CORE, [(0, 1), (1, 0)])


def table_rows(freq_table):
    sizes = [lax.axis_size(a) for a in (Z, Y, CORE)]
    freq = freq_table.reshape(*sizes, -1).transpose(2, 1, 0, 3)
    freq = jnp.broadcast_to(freq[:, :, :, None, :], (*freq.shape[:3], 2, freq.shape[3]))
    part = lax.broadcasted_iota(jnp.int32, freq.shape, 3)
    here = lax.axis_index(CORE)
    freq = jnp.where(here == 0, freq[::-1], freq)
    return freq.reshape(-1, 1), part.reshape(-1, 1)


def per_device(velocity, radiation_modes, resistance, mode_ranks, freq_table):
    mode_count = lax.axis_size(MODE)
    width = radiation_modes.shape[1]
    basis = exchange(radiation_modes.reshape(mode_count, -1, width), MODE)
    freq, part = table_rows(freq_table)
    table, spectra = make_spectra(freq, part, velocity[0])
    received = swap_cores(make_partial(spectra, basis, 0))
    own = make_partial(spectra, basis, 1)
    coef = (own.astype(F32) + received.astype(F32)).astype(BF16)
    coef = reduced(coef, Y)
    coef = reduced(coef, Z)
    coef = spread(coef, MODE)
    offset = (lax.axis_index(MODE) * width).reshape(1)
    forcing = make_forcing(mode_ranks, offset, coef, resistance[0])
    forcing = spread(forcing, Z)
    forcing = spread(forcing.reshape(-1, width), (MODE, Y))
    forcing = forcing.reshape(mode_count, -1, width)
    received = swap_cores(forcing)
    history = make_history(basis, forcing, table, 1, None, F32)
    history = make_history(basis, received, table, 0, history, BF16)
    return history[None]


def solution(mesh):
    torus = Mesh(mesh.devices.reshape(16, 4, 2, mesh.shape["mode"]), (Z, Y, CORE, MODE))
    bands = (Z, Y, CORE)
    patches = (Z, Y, CORE, MODE)
    in_specs = (P(None, patches, None), P(bands, MODE), P(bands, None, MODE), P(bands), P())
    return jax.shard_map(
        per_device, mesh=torus, in_specs=in_specs, out_specs=P(None, patches, None), check_vma=False
    )
```

time: 228 us -> 141 us (0.62)
  waiting for transfers between devices: 79.9 us -> 6.89 us
  Pallas kernels: 0 us -> 20.9 us
  between operations: 14.2 us -> 0.77 us
  matrix products: 9.44 us -> 0 us
  local copies, waits for them, and re-layouts: 16.6 us -> 8.06 us
  other arithmetic: 9.64 us -> 1.91 us
  blocking collectives: 70 us -> 77.2 us
  starting transfers between devices: 28 us -> 24.9 us
    all_gather x2 -> x0, waiting for transfers between devices: 45.7 us -> none  [gather_in_order(): parts = lax.all_gather(parts, axes[k])]
    all_to_all x2 -> x4, blocking collectives: 36.9 us -> 77.2 us  [exchange(): return lax.all_to_all(value, axis, split_axis=0, concat_axis=0, tiled=True)]
    all_gather x2 -> x0, blocking collectives: 33.1 us -> none  [gather_in_order(): parts = lax.all_gather(parts, axes[k])]
    all_to_all x2, waiting for transfers between devices: 34.2 us -> 3.82 us  [exchange(): return lax.all_to_all(value, axis, split_axis=0, concat_axis=0, tiled=True)]
    pallas_call x0 -> x6, Pallas kernels: none -> 20.9 us  [the longest x1 17 us: make_spectra(): call(functools.partial(spectra_kernel, steps), (jax.ShapeDtypeStruct((row...]
    all_to_all x2, starting transfers between devices: 27.9 us -> 9.36 us  [exchange(): return lax.all_to_all(value, axis, split_axis=0, concat_axis=0, tiled=True)]
    ppermute x0 -> x2, starting transfers between devices: none -> 15.6 us  [swap_cores(): return lax.ppermute(value, CORE, [(0, 1), (1, 0)])]
    dot_general x4 -> x0, matrix products: 9.44 us -> none  [the longest x1 6.13 us: per_device(): jnp.einsum('wpcf,tcf->wpt', surface_force, dft_table, preferred_element_t...]
  transfers between devices with their start and end apart: 4 -> 4, of which waited for: 4 -> 3; matrix products, arithmetic and copies ran while one was open for 1% -> 2% of each run, Pallas kernels for 0% -> 13%
where the time goes in v1:
time: 141 us
  blocking collectives  77.2 us (55%)
  starting transfers between devices  24.9 us (18%)
  Pallas kernels  20.9 us (15%)
  local copies, waits for them, and re-layouts  8.06 us (6%)
  waiting for transfers between devices  6.89 us (5%)
  other arithmetic  1.91 us (1%)
    all_to_all x4, blocking collectives, exchange(): return lax.all_to_all(value, axis, split_axis=0, concat_axis=0, tiled=True)  77.2 us
    pallas_call x1, Pallas kernels, make_spectra(): call(functools.partial(spectra_kernel, steps), (jax.ShapeDtypeStruct((row...  17 us
    ppermute x2, starting transfers between devices, swap_cores(): return lax.ppermute(value, CORE, [(0, 1), (1, 0)])  15.6 us
    all_to_all x2, starting transfers between devices, exchange(): return lax.all_to_all(value, axis, split_axis=0, concat_axis=0, tiled=True)  9.36 us
    unnamed x8, local copies, waits for them, and re-layouts  4.35 us
    all_to_all x2, waiting for transfers between devices, exchange(): return lax.all_to_all(value, axis, split_axis=0, concat_axis=0, tiled=True)  3.82 us
    ppermute x2, waiting for transfers between devices, swap_cores(): return lax.ppermute(value, CORE, [(0, 1), (1, 0)])  3.06 us
  transfers between devices with their start and end apart: 4, of which 3 were waited for; matrix products, arithmetic and copies ran while one was open for 2% of the time, Pallas kernels for 13%

profile of v1, /device:TPU:1, one launch (start us, length us, event | category | flops | bytes accessed | tf_op | source)
XLA Modules:
  0.0 140.7 jit_solution(4086647028524129860)
XLA Ops:
  0.0 4.8 %all-to-all-start = ((bf16[4,256,256]{2,1,0:T(8,128)(2,1)}), bf16[4,256,256]{2,1,0:T(8,128)(2,1)S(1)}, u32[]{:S(2)}, u32[]{:S(2)}) async-start(bf16[4,256,256]{2,1,0:T(8,128)(2,1)} %bitcast.16), calls=%async_computation | async-start | bytes 1048576 | tf_op jit(solution)/shard_map/all_to_all | solution.py:159
  4.8 0.8 reshape.30
  5.8 1.0 reshape.37.freq_ref
  6.9 1.0 reshape.38.part_ref
  7.9 1.0 copy-done.1
  8.9 1.0 copy-done.2
  10.0 1.0 copy-done.3
  11.0 17.0 %shard_map.55 = (bf16[1024,1024]{1,0:T(8,128)(2,1)S(1)}, bf16[1024,256]{1,0:T(8,128)(2,1)S(1)}) custom-call(s32[1024,1]{1,0:T(8,128)S(1)} %copy-done.1, s32[1024,1]{1,0:T(8,128)S(1)} %copy-done.2, bf16[256,1024]{1,0:T(8,128)(2,1)S(1)} %bitcast.13), custom_call_target="tpu_custom_call" | custom-call | flops 536870912 | bytes 4194304 | tf_op jit(solution)/shard_map/pallas_call | solution.py:58
  28.7 7.4 %collective-permute-start = (bf16[512,1024]{1,0:T(8,128)(2,1)S(1)}, bf16[512,1024]{1,0:T(8,128)(2,1)S(1)}, u32[]{:S(2)}, u32[]{:S(2)}) collective-permute-start(bf16[512,1024]{1,0:T(8,128)(2,1)S(1)} %shard_map.57), channel_id=1, source_target_pairs={{0,4},{4,0},{1,5},{5,1},{2,6},{6,2},{3,7},{7,3},{8,12},{12,8},{9,1... | collective-permute-start | bytes 3145736 | tf_op jit(solution)/shard_map/ppermute | solution.py:173
  36.1 0.6 shard_map.56
  36.8 1.6 %collective-permute-done = bf16[512,1024]{1,0:T(8,128)(2,1)S(1)} collective-permute-done((bf16[512,1024]{1,0:T(8,128)(2,1)S(1)}, bf16[512,1024]{1,0:T(8,128)(2,1)S(1)}, u32[]{:S(2)}, u32[]{:S(2)}) %collective-permute-start) | collective-permute-done | bytes 1048608 | tf_op jit(solution)/shard_map/ppermute | solution.py:173
  38.8 18.0 %all_to_all.30 = bf16[4,128,1024]{2,1,0:T(8,128)(2,1)} all-to-all(bf16[4,128,1024]{2,1,0:T(8,128)(2,1)S(1)} %bitcast.14), channel_id=1, replica_groups=mesh['band_0'=16,'band_1'=4,'band_2'=2,'mode'=4] {'band_1'}, dimensions={0} | all-to-all | bytes 2097152 | tf_op jit(solution)/shard_map/all_to_all | solution.py:159
  56.8 1.4 %reduce_sum.24 = bf16[128,1024]{1,0:T(8,128)(2,1)S(1)} reduce(bf16[4,128,1024]{2,1,0:T(8,128)(2,1)} %all_to_all.30, bf16[]{:T(256)} %constant.16.clone.1), dimensions={0}, to_apply=%region_0.1 | reduce | flops 393216 | bytes 1310722 | tf_op jit(solution)/shard_map/reduce_sum | solution.py:169
  58.2 23.3 %all_to_all.31 = bf16[16,8,1024]{2,1,0:T(8,128)(2,1)S(1)} all-to-all(bf16[16,8,1024]{2,1,0:T(8,128)(2,1)S(1)} %bitcast.15), channel_id=1, replica_groups=mesh['band_0'=16,'band_1'=4,'band_2'=2,'mode'=4] {'band_0'}, dimensions={0} | all-to-all | bytes 524288 | tf_op jit(solution)/shard_map/all_to_all | solution.py:159
  81.5 0.6 broadcast_in_dim.19
  82.2 4.5 %all-to-all-start.3 = ((bf16[4,8,1024]{2,1,0:T(8,128)(2,1)}), bf16[4,8,1024]{2,1,0:T(8,128)(2,1)S(1)}, u32[]{:S(2)}, u32[]{:S(2)}) async-start(bf16[4,8,1024]{2,1,0:T(8,128)(2,1)} %broadcast_in_dim.19), calls=%async_computation.3 | async-start | bytes 131072 | tf_op jit(solution)/shard_map/all_to_all | solution.py:159
  87.4 3.8 %all-to-all-done.3.coef_ref = bf16[4,8,1024]{2,1,0:T(8,128)(2,1)S(1)} async-done(((bf16[4,8,1024]{2,1,0:T(8,128)(2,1)}), bf16[4,8,1024]{2,1,0:T(8,128)(2,1)S(1)}, u32[]{:S(2)}, u32[]{:S(2)}) %all-to-all-start.3) | async-done | bytes 65568 | tf_op jit(solution)/shard_map/all_to_all | solution.py:159
  91.2 1.2 copy-done
  92.6 21.3 %all_to_all.32 = bf16[16,8,256]{2,1,0:T(8,128)(2,1)S(1)} all-to-all(bf16[16,8,256]{2,1,0:T(8,128)(2,1)S(1)} %broadcast_in_dim.20), channel_id=1, replica_groups=mesh['band_0'=16,'band_1'=4,'band_2'=2,'mode'=4] {'band_0'}, dimensions={0} | all-to-all | bytes 131072 | tf_op jit(solution)/shard_map/all_to_all | solution.py:159
  114.0 14.7 %all_to_all.33 = bf16[16,128,256]{2,1,0:T(8,128)(2,1)S(1)} all-to-all(bf16[16,128,256]{2,1,0:T(8,128)(2,1)S(1)} %broadcast_in_dim.21), channel_id=1, replica_groups=mesh['band_0'=16,'band_1'=4,'band_2'=2,'mode'=4] {'mode','band_1'}, dimensions={0} | all-to-all | bytes 2097152 | tf_op jit(solution)/shard_map/all_to_all | solution.py:159
  128.7 8.2 %collective-permute-start.1 = (bf16[4,512,256]{2,1,0:T(8,128)(2,1)S(1)}, bf16[4,512,256]{2,1,0:T(8,128)(2,1)S(1)}, u32[]{:S(2)}, u32[]{:S(2)}) collective-permute-start(bf16[4,512,256]{2,1,0:T(8,128)(2,1)S(1)} %bitcast.10), channel_id=1, source_target_pairs={{0,4},{4,0},{1,5},{5,1},{2,6},{6,2},{3,7},{7,3},{8,12},{12,8},{9,1... | collective-permute-start | bytes 3145736 | tf_op jit(solution)/shard_map/ppermute | solution.py:173
  136.8 0.8 shard_map.59.rest_0_
  137.7 1.4 %collective-permute-done.1.forcing_ref = bf16[4,512,256]{2,1,0:T(8,128)(2,1)S(1)} collective-permute-done((bf16[4,512,256]{2,1,0:T(8,128)(2,1)S(1)}, bf16[4,512,256]{2,1,0:T(8,128)(2,1)S(1)}, u32[]{:S(2)}, u32[]{:S(2)}) %collective-permute-start.1) | collective-permute-done | bytes 1048608 | tf_op jit(solution)/shard_map/ppermute | solution.py:173
  139.1 1.6 %shard_map.60 = bf16[256,1024]{1,0:T(8,128)(2,1)} custom-call(bf16[4,256,256]{2,1,0:T(8,128)(2,1)S(1)} %all-to-all-done.basis_ref, bf16[4,512,256]{2,1,0:T(8,128)(2,1)S(1)} %collective-permute-done.1.forcing_ref, bf16[1024,1024]{1,0:T(8,128)(2,1)S(1)} %get-tuple-element.8.table_ref, f32[256,1024]{1,0:T(8,128)S(1)} %shard_map.59.rest_0_), custom_call_target="tpu_custom_call" | custom-call | flops 536870912 | bytes 4194304 | tf_op jit(solution)/shard_map/pallas_call | solution.py:143
  (15 shorter events, 1.5 us)
Async XLA Ops:
  0.0 28.1 %all-to-all-start = ((bf16[4,256,256]{2,1,0:T(8,128)(2,1)}), bf16[4,256,256]{2,1,0:T(8,128)(2,1)S(1)}, u32[]{:S(2)}, u32[]{:S(2)}) async-start(bf16[4,256,256]{2,1,0:T(8,128)(2,1)} %bitcast.16), calls=%async_computation | async-start | bytes 1048576 | tf_op jit(solution)/shard_map/all_to_all | solution.py:159
  7.9 1.0 copy-start.1
  8.9 1.0 copy-start.2
  10.0 1.0 copy-start.3
  28.7 9.7 %collective-permute-start = (bf16[512,1024]{1,0:T(8,128)(2,1)S(1)}, bf16[512,1024]{1,0:T(8,128)(2,1)S(1)}, u32[]{:S(2)}, u32[]{:S(2)}) collective-permute-start(bf16[512,1024]{1,0:T(8,128)(2,1)S(1)} %shard_map.57), channel_id=1, source_target_pairs={{0,4},{4,0},{1,5},{5,1},{2,6},{6,2},{3,7},{7,3},{8,12},{12,8},{9,1... | collective-permute-start | bytes 3145736 | tf_op jit(solution)/shard_map/ppermute | solution.py:173
  82.2 9.0 %all-to-all-start.3 = ((bf16[4,8,1024]{2,1,0:T(8,128)(2,1)}), bf16[4,8,1024]{2,1,0:T(8,128)(2,1)S(1)}, u32[]{:S(2)}, u32[]{:S(2)}) async-start(bf16[4,8,1024]{2,1,0:T(8,128)(2,1)} %broadcast_in_dim.19), calls=%async_computation.3 | async-start | bytes 131072 | tf_op jit(solution)/shard_map/all_to_all | solution.py:159
  91.2 1.2 copy-start
  128.7 10.4 %collective-permute-start.1 = (bf16[4,512,256]{2,1,0:T(8,128)(2,1)S(1)}, bf16[4,512,256]{2,1,0:T(8,128)(2,1)S(1)}, u32[]{:S(2)}, u32[]{:S(2)}) collective-permute-start(bf16[4,512,256]{2,1,0:T(8,128)(2,1)S(1)} %bitcast.10), channel_id=1, source_target_pairs={{0,4},{4,0},{1,5},{5,1},{2,6},{6,2},{3,7},{7,3},{8,12},{12,8},{9,1... | collective-permute-start | bytes 3145736 | tf_op jit(solution)/shard_map/ppermute | solution.py:173

commit v2 on v1

v2 whole, which is shorter than its diff:
```python
import functools
import math

import jax
import jax.numpy as jnp
from jax import lax
from jax.experimental import pallas as pl
from jax.experimental.pallas import tpu as pltpu
from jax.sharding import Mesh
from jax.sharding import PartitionSpec as P

Z, Y, CORE, MODE = "band_0", "band_1", "band_2", "mode"
F32, BF16, I32 = jnp.float32, jnp.bfloat16, jnp.int32
LANES = 128
VMEM_BYTES = 24 * 1024 * 1024
SMEM = pl.BlockSpec(memory_space=pltpu.SMEM)
WHOLE = pl.BlockSpec(memory_space=pltpu.VMEM)


def shape(dims, dtype):
    return jax.ShapeDtypeStruct(tuple(dims), dtype)


def call(kernel, out_shape, flops, **options):
    return pl.pallas_call(
        kernel,
        out_shape=out_shape,
        compiler_params=pltpu.CompilerParams(vmem_limit_bytes=VMEM_BYTES),
        cost_estimate=pl.CostEstimate(flops=flops, bytes_accessed=1 << 20, transcendentals=0),
        **options,
    )


def dot(a, b):
    return jnp.dot(a, b, preferred_element_type=F32)


def dot_t(a, b):
    return lax.dot_general(a, b, (((1,), (1,)), ((), ())), preferred_element_type=F32)


def sin_cos(phase, steps):
    quadrant = (phase + steps // 8) >> (int(math.log2(steps)) - 2)
    x = (phase - quadrant * (steps // 4)).astype(F32) * (2.0 * math.pi / steps)
    y = x * x
    sin = x * (1.0 + y * (-1 / 6 + y * (1 / 120 + y * (-1 / 5040 + y * (1 / 362880)))))
    cos = 1.0 + y * (-1 / 2 + y * (1 / 24 + y * (-1 / 720 + y * (1 / 40320 - y * (1 / 3628800)))))
    odd = (quadrant & 1) == 1
    sign_sin = jnp.where((quadrant & 2) == 2, -1.0, 1.0)
    sign_cos = jnp.where(((quadrant + 1) & 2) == 2, -1.0, 1.0)
    return jnp.where(odd, cos, sin) * sign_sin, jnp.where(odd, sin, cos) * sign_cos


def cos_eighth(k):
    size = jnp.where((k & 1) == 1, math.sqrt(0.5), jnp.where((k & 2) == 2, 0.0, 1.0))
    return jnp.where(((k + 1) & 4) == 4, -size, size)


def spectra_kernel(
    z_count, y_count, slots, core_ref, freq_ref, velocity_ref, matrix_ref, table_ref, out_ref, rounded_ref
):
    rows, steps = table_ref.shape
    all_slots = freq_ref.shape[1]
    row = lax.broadcasted_iota(I32, (rows, all_slots), 0)
    source = (row // (2 * slots) * y_count + pl.program_id(0)) * (2 * slots)
    source = source + core_ref[0] * slots + (row & (slots - 1))
    lane = lax.broadcasted_iota(I32, (rows, all_slots), 1)
    freq = jnp.where(lane == source, freq_ref[...].astype(F32), 0.0)
    freq = jnp.sum(freq, axis=1, keepdims=True).astype(I32)
    freq = jnp.broadcast_to(freq, (rows, LANES))
    row = lax.broadcasted_iota(I32, (rows, LANES), 0)
    low = lax.broadcasted_iota(I32, (rows, LANES), 1)
    imaginary = (row // slots) & 1
    phase = (low * freq + imaginary * (steps // 4)) & (steps - 1)
    sin_low, cos_low = sin_cos(phase, steps)
    norming = 1.0 / math.sqrt(steps)
    sin_low, cos_low = sin_low * norming, cos_low * norming
    for high in range(steps // LANES):
        eighth = (freq * (high * LANES * 8 // steps)) & 7
        piece = cos_low * cos_eighth(eighth) - sin_low * cos_eighth((eighth + 6) & 7)
        table_ref[:, high * LANES : (high + 1) * LANES] = piece.astype(BF16)
    out_ref[...] = dot_t(table_ref[...], velocity_ref[...]).astype(BF16)
    rounded_ref[...] = matrix_ref[...].astype(BF16)


def make_spectra(core, freq_table, velocity, matrix):
    z_count, y_count = lax.axis_size(Z), lax.axis_size(Y)
    all_slots = freq_table.shape[0]
    slots = all_slots // (z_count * y_count * lax.axis_size(CORE))
    patches, steps = velocity.shape
    assert 8 * LANES == steps and slots & (slots - 1) == 0
    tile = z_count * 2 * slots
    rows = tile * y_count
    depth, width = matrix.shape
    return call(
        functools.partial(spectra_kernel, z_count, y_count, slots),
        (shape((rows, steps), BF16), shape((rows, patches), BF16), shape((depth, width), BF16)),
        2 * rows * patches * steps,
        grid=(y_count,),
        in_specs=[
            SMEM,
            pl.BlockSpec((1, all_slots), lambda i: (0, 0)),
            pl.BlockSpec((patches, steps), lambda i: (0, 0)),
            pl.BlockSpec((depth // y_count, width), lambda i: (i, 0)),
        ],
        out_specs=(
            pl.BlockSpec((tile, steps), lambda i: (i, 0)),
            pl.BlockSpec((tile, patches), lambda i: (i, 0)),
            pl.BlockSpec((depth // y_count, width), lambda i: (i, 0)),
        ),
    )(core, freq_table.reshape(1, -1), velocity, matrix)


def other_kernel(table_ref, velocity_ref, out_ref):
    out_ref[...] = dot_t(table_ref[...], velocity_ref[...]).astype(BF16)


def other_spectra(table, velocity):
    rows, patches = table.shape[0], velocity.shape[0]
    return call(
        other_kernel,
        shape((rows, patches), BF16),
        2 * rows * velocity.size,
        in_specs=[WHOLE, WHOLE],
        out_specs=WHOLE,
    )(table, velocity)


def partial_kernel(spectra_ref, basis_ref, *rest):
    out_ref = rest[-1]
    value = dot(spectra_ref[...], basis_ref[0])
    if len(rest) > 1:
        value = value + rest[0][0]
    out_ref[0] = value.astype(out_ref.dtype)


def make_partial(spectra, basis, before, dtype):
    rows, patches = spectra.shape
    parts, _, width = basis.shape
    more = [] if before is None else [before]
    return call(
        partial_kernel,
        shape((parts, rows, width), dtype),
        2 * rows * patches * parts * width,
        grid=(parts,),
        in_specs=[
            pl.BlockSpec((rows, patches), lambda i: (0, 0)),
            pl.BlockSpec((1, patches, width), lambda i: (i, 0, 0)),
        ]
        + [pl.BlockSpec((1, rows, width), lambda i: (i, 0, 0)) for _ in more],
        out_specs=pl.BlockSpec((1, rows, width), lambda i: (i, 0, 0)),
    )(spectra, basis, *more)


def added(parts_ref):
    total = parts_ref[0].astype(F32)
    for k in range(1, parts_ref.shape[0]):
        total = total + parts_ref[k].astype(F32)
    return total


def sum_kernel(parts_ref, out_ref):
    out_ref[...] = added(parts_ref).astype(BF16)


def summed(parts):
    return call(
        sum_kernel, shape(parts.shape[1:], BF16), parts.size, in_specs=[WHOLE], out_specs=WHOLE
    )(parts)


def kept(value, rank_ref, offset_ref):
    index = lax.broadcasted_iota(I32, value.shape, 1) + offset_ref[0]
    return jnp.where(index < rank_ref[0], value, 0.0)


def coefficients_kernel(rank_ref, offset_ref, parts_ref, out_ref):
    value = kept(added(parts_ref), rank_ref, offset_ref).astype(BF16)
    out_ref[...] = jnp.broadcast_to(value, out_ref.shape)


def make_coefficients(rank, offset, parts, copies):
    return call(
        coefficients_kernel,
        shape((copies, *parts.shape[1:]), BF16),
        parts.size,
        in_specs=[SMEM, SMEM, WHOLE],
        out_specs=WHOLE,
    )(rank, offset, parts)


def forcing_kernel(rank_ref, offset_ref, coef_ref, matrix_ref, out_ref):
    width = coef_ref.shape[2]
    total = dot(coef_ref[0], matrix_ref[:width])
    for k in range(1, coef_ref.shape[0]):
        total = total + dot(coef_ref[k], matrix_ref[k * width : (k + 1) * width])
    value = kept(2.0 * total, rank_ref, offset_ref).astype(BF16)
    out_ref[...] = jnp.broadcast_to(value, out_ref.shape)


def make_forcing(rank, offset, coef, matrix, copies):
    rows = coef.shape[1]
    return call(
        forcing_kernel,
        shape((copies, rows, matrix.shape[1]), BF16),
        2 * rows * matrix.size,
        in_specs=[SMEM, SMEM, WHOLE, WHOLE],
        out_specs=WHOLE,
    )(rank, offset, coef, matrix)


def history_kernel(basis_ref, forcing_ref, table_ref, out_ref):
    total = dot_t(basis_ref[0], forcing_ref[0])
    for k in range(1, basis_ref.shape[0]):
        total = total + dot_t(basis_ref[k], forcing_ref[k])
    out_ref[...] = dot(total.astype(BF16), table_ref[...]).astype(out_ref.dtype)


def make_history(basis, forcing, table, dtype):
    parts, patches, width = basis.shape
    rows, steps = table.shape
    return call(
        history_kernel,
        shape((patches, steps), dtype),
        2 * rows * patches * (steps + parts * width),
        in_specs=[WHOLE, WHOLE, WHOLE],
        out_specs=WHOLE,
    )(basis, forcing, table)


def exchange(value, axis):
    return lax.all_to_all(value, axis, split_axis=0, concat_axis=0, tiled=True)


def swap_cores(value):
    return lax.ppermute(value, CORE, [(0, 1), (1, 0)])


def per_device(velocity, radiation_modes, resistance, mode_ranks, freq_table):
    modes, ys, zs = lax.axis_size(MODE), lax.axis_size(Y), lax.axis_size(Z)
    width = radiation_modes.shape[1]
    core = lax.axis_index(CORE).reshape(1)
    offset = (lax.axis_index(MODE) * width).reshape(1)
    basis = exchange(radiation_modes.reshape(modes, -1, width), MODE)
    velocity_other = swap_cores(velocity[0])
    table, spectra, matrix = make_spectra(core, freq_table, velocity[0], resistance[0])
    spectra_other = other_spectra(table, velocity_other)
    basis, spectra, spectra_other = lax.optimization_barrier((basis, spectra, spectra_other))
    basis_other = swap_cores(basis)
    coef = make_partial(spectra, basis, None, F32)
    coef = make_partial(spectra_other, basis_other, coef, BF16)
    coef = summed(exchange(coef.reshape(modes * ys, -1, width), (MODE, Y)))
    coef = exchange(coef.reshape(zs, -1, width), Z)
    coef = exchange(make_coefficients(mode_ranks, offset, coef, modes), MODE)
    forcing = exchange(make_forcing(mode_ranks, offset, coef, matrix, zs), Z)
    forcing = forcing.reshape(-1, width)
    forcing = exchange(jnp.broadcast_to(forcing, (modes * ys, *forcing.shape)), (MODE, Y))
    forcing = forcing.reshape(modes, -1, width)
    sent = make_history(basis_other, forcing, table, BF16)
    received = swap_cores(sent)
    history = make_history(basis, forcing, table, F32)
    return (history + received.astype(F32)).astype(BF16)[None]


def solution(mesh):
    torus = Mesh(mesh.devices.reshape(16, 4, 2, mesh.shape["mode"]), (Z, Y, CORE, MODE))
    bands = (Z, Y, CORE)
    patches = (Z, Y, CORE, MODE)
    in_specs = (P(None, patches, None), P(bands, MODE), P(bands, None, MODE), P(bands), P())
    return jax.shard_map(
        per_device, mesh=torus, in_specs=in_specs, out_specs=P(None, patches, None), check_vma=False
    )
```

time: 141 us -> 119 us (0.84)
  blocking collectives: 77.2 us -> 54.3 us
  Pallas kernels: 20.9 us -> 8.44 us
  starting transfers between devices: 24.9 us -> 36.2 us
  waiting for transfers between devices: 6.89 us -> 14.9 us
  local copies, waits for them, and re-layouts: 8.06 us -> 3.03 us
    all_to_all x4, blocking collectives: 77.2 us -> 54.3 us  [exchange(): return lax.all_to_all(value, axis, split_axis=0, concat_axis=0, tiled=True)]
    pallas_call x6 -> x9, Pallas kernels: 20.9 us -> 8.44 us  [the longest x1 3.49 us: make_spectra(): call(functools.partial(spectra_kernel, z_count, y_count, slots), (shape((...]
    all_to_all x2, waiting for transfers between devices: 3.82 us -> 13.7 us  [exchange(): return lax.all_to_all(value, axis, split_axis=0, concat_axis=0, tiled=True)]
    all_to_all x2, starting transfers between devices: 9.36 us -> 15.8 us  [exchange(): return lax.all_to_all(value, axis, split_axis=0, concat_axis=0, tiled=True)]
    ppermute x2 -> x3, starting transfers between devices: 15.6 us -> 20.5 us  [swap_cores(): return lax.ppermute(value, CORE, [(0, 1), (1, 0)])]
    reshape x3 -> x0, local copies, waits for them, and re-layouts: 2.87 us -> none  [the longest x2 2.05 us: table_rows(): return (freq.reshape(-1, 1), part.reshape(-1, 1))]
    ppermute x2 -> x3, waiting for transfers between devices: 3.06 us -> 1.26 us  [swap_cores(): return lax.ppermute(value, CORE, [(0, 1), (1, 0)])]
    reduce_sum x2 -> x0, other arithmetic: 1.47 us -> none  [reduced(): return jnp.sum(parts.astype(F32), axis=0).astype(BF16)]
  transfers between devices with their start and end apart: 4 -> 5, of which waited for: 3 -> 4; matrix products, arithmetic and copies ran while one was open for 2% -> 0% of each run, Pallas kernels for 13% -> 5%
where the time goes in v2:
time: 119 us
  blocking collectives  54.3 us (46%)
  starting transfers between devices  36.2 us (30%)
  waiting for transfers between devices  14.9 us (13%)
  Pallas kernels  8.44 us (7%)
  local copies, waits for them, and re-layouts  3.03 us (3%)
    all_to_all x4, blocking collectives, exchange(): return lax.all_to_all(value, axis, split_axis=0, concat_axis=0, tiled=True)  54.3 us
    ppermute x3, starting transfers between devices, swap_cores(): return lax.ppermute(value, CORE, [(0, 1), (1, 0)])  20.5 us
    all_to_all x2, starting transfers between devices, exchange(): return lax.all_to_all(value, axis, split_axis=0, concat_axis=0, tiled=True)  15.8 us
    all_to_all x2, waiting for transfers between devices, exchange(): return lax.all_to_all(value, axis, split_axis=0, concat_axis=0, tiled=True)  13.7 us
    pallas_call x1, Pallas kernels, make_spectra(): call(functools.partial(spectra_kernel, z_count, y_count, slots), (shape((...  3.49 us
    unnamed x6, local copies, waits for them, and re-layouts  2.94 us
  transfers between devices with their start and end apart: 5, of which 4 were waited for; matrix products, arithmetic and copies ran while one was open for 0% of the time, Pallas kernels for 5%

profile of v2, /device:TPU:1, one launch (start us, length us, event | category | flops | bytes accessed | tf_op | source)
XLA Modules:
  0.0 118.7 jit_solution(11590679273814412384)
XLA Ops:
  0.0 8.8 %collective-permute-start = (bf16[256,1024]{1,0:T(8,128)(2,1)}, bf16[256,1024]{1,0:T(8,128)(2,1)S(1)}, u32[]{:S(2)}, u32[]{:S(2)}) collective-permute-start(bf16[256,1024]{1,0:T(8,128)(2,1)} %bitcast.16), channel_id=1, source_target_pairs={{0,4},{4,0},{1,5},{5,1},{2,6},{6,2},{3,7},{7,3},{8,12},{12,8},{9,1... | collective-permute-start | bytes 1572872 | tf_op jit(solution)/shard_map/ppermute | solution.py:236
  8.8 3.5 %all-to-all-start = ((bf16[4,256,256]{2,1,0:T(8,128)(2,1)}), bf16[4,256,256]{2,1,0:T(8,128)(2,1)S(1)}, u32[]{:S(2)}, u32[]{:S(2)}) async-start(bf16[4,256,256]{2,1,0:T(8,128)(2,1)} %bitcast.19), calls=%async_computation | async-start | bytes 1048576 | tf_op jit(solution)/shard_map/all_to_all | solution.py:232
  12.3 1.2 %copy-done = f32[1,1024,256]{2,1,0:T(8,128)S(1)} copy-done((f32[1,1024,256]{2,1,0:T(8,128)S(1)}, f32[1,1024,256]{2,1,0:T(8,128)}, u32[]{:S(2)}) %copy-start) | copy-done | bytes 1048600
  13.5 1.0 copy-done.1
  14.5 0.7 copy-done.2
  15.2 3.5 %shard_map.55 = (bf16[512,1024]{1,0:T(8,128)(2,1)S(1)}, bf16[512,256]{1,0:T(8,128)(2,1)S(1)}, bf16[1024,256]{1,0:T(8,128)(2,1)S(1)}) custom-call(s32[1]{0:T(128)} %bitcast.1.core_ref, s32[1,512]{1,0:T(1,128)S(1)} %bitcast.18, bf16[256,1024]{1,0:T(8,128)(2,1)S(1)} %bitcast.17, f32[1024,256]{1,0:T(8,128)S(1)} %bitcast.15), custom_call_target="tpu_custom_call" | custom-call | flops 268435456 | bytes 1048576 | tf_op jit(solution)/shard_map/pallas_call | solution.py:95
  18.7 0.5 shard_map.56.spectra_ref
  19.2 2.7 %all-to-all-done.basis_ref = bf16[4,256,256]{2,1,0:T(8,128)(2,1)S(1)} async-done(((bf16[4,256,256]{2,1,0:T(8,128)(2,1)}), bf16[4,256,256]{2,1,0:T(8,128)(2,1)S(1)}, u32[]{:S(2)}, u32[]{:S(2)}) %all-to-all-start) | async-done | bytes 524320 | tf_op jit(solution)/shard_map/all_to_all | solution.py:232
  21.9 2.7 %collective-permute-start.1 = (bf16[4,256,256]{2,1,0:T(8,128)(2,1)S(1)}, bf16[4,256,256]{2,1,0:T(8,128)(2,1)S(1)}, u32[]{:S(2)}, u32[]{:S(2)}) collective-permute-start(bf16[4,256,256]{2,1,0:T(8,128)(2,1)S(1)} %all-to-all-done.basis_ref), channel_id=1, source_target_pairs={{0,4},{4,0},{1,5},{5,1},{2,6},{6,2},{3,7},{7,3},{8,12},{12,8},{9,1... | collective-permute-start | bytes 1572872 | tf_op jit(solution)/shard_map/ppermute | solution.py:236
  24.6 0.9 shard_map.57.rest_0_
  25.5 0.6 collective-permute-done.1.basis_ref
  26.1 0.9 shard_map.58
  27.0 18.5 %all_to_all.30.parts_ref = bf16[16,128,256]{2,1,0:T(8,128)(2,1)S(1)} all-to-all(bf16[16,128,256]{2,1,0:T(8,128)(2,1)S(1)} %bitcast.14), channel_id=1, replica_groups=mesh['band_0'=16,'band_1'=4,'band_2'=2,'mode'=4] {'mode','band_1'}, dimensions={0} | all-to-all | bytes 2097152 | tf_op jit(solution)/shard_map/all_to_all | solution.py:232
  45.5 0.8 shard_map.59
  46.3 12.3 %all-to-all-start.2 = ((bf16[16,8,256]{2,1,0:T(8,128)(2,1)}), bf16[16,8,256]{2,1,0:T(8,128)(2,1)S(1)}, u32[]{:S(2)}, u32[]{:S(2)}) async-start(bf16[16,8,256]{2,1,0:T(8,128)(2,1)} %bitcast.7), calls=%async_computation.2 | async-start | bytes 131072 | tf_op jit(solution)/shard_map/all_to_all | solution.py:232
  59.3 11.0 %all-to-all-done.2.parts_ref = bf16[16,8,256]{2,1,0:T(8,128)(2,1)S(1)} async-done(((bf16[16,8,256]{2,1,0:T(8,128)(2,1)}), bf16[16,8,256]{2,1,0:T(8,128)(2,1)S(1)}, u32[]{:S(2)}, u32[]{:S(2)}) %all-to-all-start.2) | async-done | bytes 65568 | tf_op jit(solution)/shard_map/all_to_all | solution.py:232
  70.3 6.6 %all_to_all.31.coef_ref = bf16[4,8,256]{2,1,0:T(8,128)(2,1)S(1)} all-to-all(bf16[4,8,256]{2,1,0:T(8,128)(2,1)S(1)} %shard_map.60), channel_id=1, replica_groups=mesh['band_0'=16,'band_1'=4,'band_2'=2,'mode'=4] {'mode'}, dimensions={0} | all-to-all | bytes 32768 | tf_op jit(solution)/shard_map/all_to_all | solution.py:232
  77.0 14.3 %all_to_all.32 = bf16[16,8,256]{2,1,0:T(8,128)(2,1)S(1)} all-to-all(bf16[16,8,256]{2,1,0:T(8,128)(2,1)S(1)} %shard_map.61), channel_id=1, replica_groups=mesh['band_0'=16,'band_1'=4,'band_2'=2,'mode'=4] {'band_0'}, dimensions={0} | all-to-all | bytes 131072 | tf_op jit(solution)/shard_map/all_to_all | solution.py:232
  91.4 14.9 %all_to_all.33 = bf16[16,128,256]{2,1,0:T(8,128)(2,1)S(1)} all-to-all(bf16[16,128,256]{2,1,0:T(8,128)(2,1)S(1)} %broadcast_in_dim.6), channel_id=1, replica_groups=mesh['band_0'=16,'band_1'=4,'band_2'=2,'mode'=4] {'mode','band_1'}, dimensions={0} | all-to-all | bytes 2097152 | tf_op jit(solution)/shard_map/all_to_all | solution.py:232
  106.4 0.8 shard_map.63
  107.2 9.0 %collective-permute-start.2 = (bf16[256,1024]{1,0:T(8,128)(2,1)S(1)}, bf16[256,1024]{1,0:T(8,128)(2,1)S(1)}, u32[]{:S(2)}, u32[]{:S(2)}) collective-permute-start(bf16[256,1024]{1,0:T(8,128)(2,1)S(1)} %shard_map.63), channel_id=1, source_target_pairs={{0,4},{4,0},{1,5},{5,1},{2,6},{6,2},{3,7},{7,3},{8,12},{12,8},{9,1... | collective-permute-start | bytes 1572872 | tf_op jit(solution)/shard_map/ppermute | solution.py:236
  116.2 0.8 shard_map.62
  117.0 0.7 collective-permute-done.2
  117.7 0.9 fusion
  (7 shorter events, 0.3 us)
Async XLA Ops:
  0.0 18.7 %collective-permute-start = (bf16[256,1024]{1,0:T(8,128)(2,1)}, bf16[256,1024]{1,0:T(8,128)(2,1)S(1)}, u32[]{:S(2)}, u32[]{:S(2)}) collective-permute-start(bf16[256,1024]{1,0:T(8,128)(2,1)} %bitcast.16), channel_id=1, source_target_pairs={{0,4},{4,0},{1,5},{5,1},{2,6},{6,2},{3,7},{7,3},{8,12},{12,8},{9,1... | collective-permute-start | bytes 1572872 | tf_op jit(solution)/shard_map/ppermute | solution.py:236
  8.8 13.1 %all-to-all-start = ((bf16[4,256,256]{2,1,0:T(8,128)(2,1)}), bf16[4,256,256]{2,1,0:T(8,128)(2,1)S(1)}, u32[]{:S(2)}, u32[]{:S(2)}) async-start(bf16[4,256,256]{2,1,0:T(8,128)(2,1)} %bitcast.19), calls=%async_computation | async-start | bytes 1048576 | tf_op jit(solution)/shard_map/all_to_all | solution.py:232
  12.3 1.2 %copy-start = (f32[1,1024,256]{2,1,0:T(8,128)S(1)}, f32[1,1024,256]{2,1,0:T(8,128)}, u32[]{:S(2)}) copy-start(f32[1,1024,256]{2,1,0:T(8,128)} %param.7) | copy-start | bytes 3145732
  13.5 1.0 copy-start.1
  14.5 0.7 copy-start.2
  21.9 4.2 %collective-permute-start.1 = (bf16[4,256,256]{2,1,0:T(8,128)(2,1)S(1)}, bf16[4,256,256]{2,1,0:T(8,128)(2,1)S(1)}, u32[]{:S(2)}, u32[]{:S(2)}) collective-permute-start(bf16[4,256,256]{2,1,0:T(8,128)(2,1)S(1)} %all-to-all-done.basis_ref), channel_id=1, source_target_pairs={{0,4},{4,0},{1,5},{5,1},{2,6},{6,2},{3,7},{7,3},{8,12},{12,8},{9,1... | collective-permute-start | bytes 1572872 | tf_op jit(solution)/shard_map/ppermute | solution.py:236
  46.3 24.0 %all-to-all-start.2 = ((bf16[16,8,256]{2,1,0:T(8,128)(2,1)}), bf16[16,8,256]{2,1,0:T(8,128)(2,1)S(1)}, u32[]{:S(2)}, u32[]{:S(2)}) async-start(bf16[16,8,256]{2,1,0:T(8,128)(2,1)} %bitcast.7), calls=%async_computation.2 | async-start | bytes 131072 | tf_op jit(solution)/shard_map/all_to_all | solution.py:232
  107.2 10.5 %collective-permute-start.2 = (bf16[256,1024]{1,0:T(8,128)(2,1)S(1)}, bf16[256,1024]{1,0:T(8,128)(2,1)S(1)}, u32[]{:S(2)}, u32[]{:S(2)}) collective-permute-start(bf16[256,1024]{1,0:T(8,128)(2,1)S(1)} %shard_map.63), channel_id=1, source_target_pairs={{0,4},{4,0},{1,5},{5,1},{2,6},{6,2},{3,7},{7,3},{8,12},{12,8},{9,1... | collective-permute-start | bytes 1572872 | tf_op jit(solution)/shard_map/ppermute | solution.py:236

commit v3 on v2

v3 whole, which is shorter than its diff:
```python
import functools
import math

import jax
import jax.numpy as jnp
from jax import lax
from jax.experimental import pallas as pl
from jax.experimental.pallas import tpu as pltpu
from jax.sharding import Mesh
from jax.sharding import PartitionSpec as P

Z, Y, CORE, MODE = "band_0", "band_1", "band_2", "mode"
F32, BF16, I32 = jnp.float32, jnp.bfloat16, jnp.int32
LANES = 128
VMEM_BYTES = 24 * 1024 * 1024
SMEM = pl.BlockSpec(memory_space=pltpu.SMEM)
WHOLE = pl.BlockSpec(memory_space=pltpu.VMEM)


def shape(dims, dtype):
    return jax.ShapeDtypeStruct(tuple(dims), dtype)


def call(kernel, out_shape, flops, bytes_accessed=1 << 20, **options):
    return pl.pallas_call(
        kernel,
        out_shape=out_shape,
        compiler_params=pltpu.CompilerParams(vmem_limit_bytes=VMEM_BYTES),
        cost_estimate=pl.CostEstimate(
            flops=flops, bytes_accessed=bytes_accessed, transcendentals=0
        ),
        **options,
    )


def dot(a, b):
    return jnp.dot(a, b, preferred_element_type=F32)


def dot_t(a, b):
    return lax.dot_general(a, b, (((1,), (1,)), ((), ())), preferred_element_type=F32)


def sin_cos(phase, steps):
    quadrant = (phase + steps // 8) >> (int(math.log2(steps)) - 2)
    x = (phase - quadrant * (steps // 4)).astype(F32) * (2.0 * math.pi / steps)
    y = x * x
    sin = x * (1.0 + y * (-1 / 6 + y * (1 / 120 + y * (-1 / 5040 + y * (1 / 362880)))))
    cos = 1.0 + y * (-1 / 2 + y * (1 / 24 + y * (-1 / 720 + y * (1 / 40320 - y * (1 / 3628800)))))
    odd = (quadrant & 1) == 1
    sign_sin = jnp.where((quadrant & 2) == 2, -1.0, 1.0)
    sign_cos = jnp.where(((quadrant + 1) & 2) == 2, -1.0, 1.0)
    return jnp.where(odd, cos, sin) * sign_sin, jnp.where(odd, sin, cos) * sign_cos


def cos_eighth(k):
    size = jnp.where((k & 1) == 1, math.sqrt(0.5), jnp.where((k & 2) == 2, 0.0, 1.0))
    return jnp.where(((k + 1) & 4) == 4, -size, size)


def make_table(slots, y_count, core, freq_in, table_ref):
    all_rows, steps = table_ref.shape
    all_slots = freq_in.shape[1]
    rows = all_rows // y_count
    cores = 2 * all_slots // all_rows
    shift = int(math.log2(slots))
    turns = steps // LANES
    norming = 1.0 / math.sqrt(steps)
    row = lax.broadcasted_iota(I32, (rows, 1), 0)
    first = (row >> (shift + 1)) * (y_count * cores * slots) + (row & (slots - 1)) + core * slots
    lane = lax.broadcasted_iota(I32, (rows, all_slots), 1)
    low = lax.broadcasted_iota(I32, (rows, LANES), 1)
    quarter = ((row >> shift) & 1) * (steps // 4)
    for y in range(y_count):
        here = slice(y * rows, (y + 1) * rows)
        freq = jnp.where(lane == first + y * cores * slots, freq_in[...].astype(F32), 0.0)
        freq = jnp.sum(freq, axis=1, keepdims=True).astype(I32)
        freq = jnp.broadcast_to(freq, (rows, LANES))
        sin, cos = sin_cos((low * freq + quarter) & (steps - 1), steps)
        sin, cos = sin * norming, cos * norming
        turn_cos, turn_sin = cos_eighth(freq & 7), cos_eighth((freq + 6) & 7)
        half_turn = jnp.where((freq & 1) == 1, -1.0, 1.0)
        for k in range(turns // 2):
            table_ref[here, k * LANES : (k + 1) * LANES] = cos.astype(BF16)
            far = k + turns // 2
            table_ref[here, far * LANES : (far + 1) * LANES] = (cos * half_turn).astype(BF16)
            cos, sin = cos * turn_cos - sin * turn_sin, sin * turn_cos + cos * turn_sin


def sent_kernel(
    slots, y_count, place_ref, freq_ref, velocity_ref, out_ref, freq_in, velocity_in, table, sems
):
    copies = [
        pltpu.make_async_copy(freq_ref, freq_in, sems.at[0]),
        pltpu.make_async_copy(velocity_ref, velocity_in, sems.at[1]),
    ]
    for copy in copies:
        copy.start()
    copies[0].wait()
    make_table(slots, y_count, 1 - place_ref[0], freq_in, table)
    copies[1].wait()
    out_ref[...] = dot_t(table[...], velocity_in[...]).astype(BF16)


def own_kernel(
    slots, y_count, place_ref, rank_ref, freq_ref, velocity_ref, matrix_ref,
    table_ref, out_ref, rounded_ref, limits_ref, matrix_in, sem,
):
    copy = pltpu.make_async_copy(matrix_ref, matrix_in, sem)
    copy.start()
    limits_ref[0] = rank_ref[0]
    limits_ref[1] = place_ref[1] * matrix_ref.shape[1]
    make_table(slots, y_count, place_ref[0], freq_ref, table_ref)
    out_ref[...] = dot_t(table_ref[...], velocity_ref[...]).astype(BF16)
    copy.wait()
    rounded_ref[...] = matrix_in[...].astype(BF16)


def in_hbm(value):
    return pltpu.with_memory_space_constraint(value, pltpu.HBM)


def make_spectra(place, rank, freq_table, velocity, matrix):
    y_count, cores = lax.axis_size(Y), lax.axis_size(CORE)
    all_slots = freq_table.shape[0]
    slots = all_slots // (lax.axis_size(Z) * y_count * cores)
    patches, steps = velocity.shape
    assert 8 * LANES == steps and slots & (slots - 1) == 0 and cores == 2
    rows = 2 * all_slots // cores
    hbm = pl.BlockSpec(memory_space=pltpu.HBM)
    table, spectra = shape((rows, steps), BF16), shape((rows, patches), BF16)
    sent, freq, velocity = call(
        functools.partial(sent_kernel, slots, y_count),
        (spectra, shape((1, all_slots), I32), shape(velocity.shape, BF16)),
        1,
        1,
        in_specs=[SMEM, hbm, hbm],
        out_specs=(WHOLE, WHOLE, WHOLE),
        scratch_shapes=[pltpu.VMEM((rows, steps), BF16), pltpu.SemaphoreType.DMA((2,))],
    )(place, in_hbm(freq_table.reshape(1, -1)), in_hbm(velocity))
    own = call(
        functools.partial(own_kernel, slots, y_count),
        (table, spectra, shape(matrix.shape, BF16), shape((2,), I32)),
        1,
        1,
        in_specs=[SMEM, SMEM, WHOLE, WHOLE, hbm],
        out_specs=(WHOLE, WHOLE, WHOLE, SMEM),
        scratch_shapes=[pltpu.VMEM(matrix.shape, F32), pltpu.SemaphoreType.DMA],
    )(place, rank, freq, velocity, in_hbm(matrix))
    return sent, *own


def partial_kernel(spectra_ref, basis_ref, before_ref, out_ref):
    for k in range(basis_ref.shape[0]):
        out_ref[k] = (dot(spectra_ref[...], basis_ref[k]) + before_ref[k]).astype(BF16)


def make_partial(spectra, basis, before):
    return call(
        partial_kernel,
        shape(before.shape, BF16),
        2 * before.size * spectra.shape[1],
        in_specs=[WHOLE] * 3,
        out_specs=WHOLE,
    )(spectra, basis, before)


def first_kernel(spectra_ref, basis_ref, out_ref):
    for k in range(basis_ref.shape[0]):
        out_ref[k] = dot(spectra_ref[...], basis_ref[k])


def first_partial(spectra, basis):
    rows, patches = spectra.shape
    parts, _, width = basis.shape
    return call(
        first_kernel,
        shape((parts, rows, width), F32),
        2 * rows * patches * parts * width,
        in_specs=[WHOLE, WHOLE],
        out_specs=WHOLE,
    )(spectra, basis)


def added(parts_ref):
    total = parts_ref[0].astype(F32)
    for k in range(1, parts_ref.shape[0]):
        total = total + parts_ref[k].astype(F32)
    return total


def sum_kernel(parts_ref, out_ref):
    out_ref[...] = added(parts_ref).astype(BF16)


def summed(parts):
    return call(
        sum_kernel, shape(parts.shape[1:], BF16), parts.size, in_specs=[WHOLE], out_specs=WHOLE
    )(parts)


def kept(value, limits_ref):
    index = lax.broadcasted_iota(I32, value.shape, 1) + limits_ref[1]
    return jnp.where(index < limits_ref[0], value, 0.0)


def coefficients_kernel(limits_ref, parts_ref, out_ref):
    value = kept(added(parts_ref), limits_ref).astype(BF16)
    out_ref[...] = jnp.broadcast_to(value, out_ref.shape)


def make_coefficients(limits, parts, copies):
    return call(
        coefficients_kernel,
        shape((copies, *parts.shape[1:]), BF16),
        parts.size,
        in_specs=[SMEM, WHOLE],
        out_specs=WHOLE,
    )(limits, parts)


def forcing_kernel(limits_ref, coef_ref, matrix_ref, out_ref):
    width = coef_ref.shape[2]
    total = dot(coef_ref[0], matrix_ref[:width])
    for k in range(1, coef_ref.shape[0]):
        total = total + dot(coef_ref[k], matrix_ref[k * width : (k + 1) * width])
    value = kept(2.0 * total, limits_ref).astype(BF16)
    out_ref[...] = jnp.broadcast_to(value, out_ref.shape)


def make_forcing(limits, coef, matrix, copies):
    rows = coef.shape[1]
    return call(
        forcing_kernel,
        shape((copies, rows, matrix.shape[1]), BF16),
        2 * rows * matrix.size,
        in_specs=[SMEM, WHOLE, WHOLE],
        out_specs=WHOLE,
    )(limits, coef, matrix)


def history_kernel(basis_ref, forcing_ref, table_ref, *rest):
    out_ref = rest[-1]
    total = dot_t(basis_ref[0], forcing_ref[0])
    for k in range(1, basis_ref.shape[0]):
        total = total + dot_t(basis_ref[k], forcing_ref[k])
    out_ref[...] = dot(total.astype(BF16), table_ref[...]).astype(out_ref.dtype)


def make_history(basis, forcing, table, dtype):
    parts, patches, width = basis.shape
    rows = forcing.shape[1]
    steps = table.shape[1]
    return call(
        history_kernel,
        shape((patches, steps), dtype),
        2 * rows * patches * (steps + parts * width),
        grid=(1,),
        in_specs=[
            pl.BlockSpec(basis.shape, lambda i: (0, 0, 0)),
            pl.BlockSpec(forcing.shape, lambda i: (0, 0, 0)),
            pl.BlockSpec((rows, steps), lambda i: (0, 0)),
        ],
        out_specs=pl.BlockSpec((patches, steps), lambda i: (0, 0)),
    )(basis, forcing, table)


def exchange(value, axis):
    return lax.all_to_all(value, axis, split_axis=0, concat_axis=0, tiled=True)


def swap_cores(value):
    return lax.ppermute(value, CORE, [(0, 1), (1, 0)])


def per_device(velocity, radiation_modes, resistance, mode_ranks, freq_table):
    modes, ys, zs = lax.axis_size(MODE), lax.axis_size(Y), lax.axis_size(Z)
    width = radiation_modes.shape[1]
    place = jnp.stack([lax.axis_index(CORE), lax.axis_index(MODE)])
    basis = exchange(radiation_modes.reshape(modes, -1, width), MODE)
    sent, table, spectra, matrix, limits = make_spectra(
        place, mode_ranks, freq_table, velocity[0], resistance[0]
    )
    spectra_other = swap_cores(sent)
    basis, spectra, spectra_other = lax.optimization_barrier((basis, spectra, spectra_other))
    basis_other = swap_cores(basis)
    coef = first_partial(spectra, basis)
    coef = make_partial(spectra_other, basis_other, coef)
    coef = summed(exchange(coef.reshape(modes * ys, -1, width), (MODE, Y)))
    coef = exchange(coef.reshape(zs, -1, width), Z)
    coef = exchange(make_coefficients(limits, coef, modes), MODE)
    forcing = exchange(make_forcing(limits, coef, matrix, zs), Z)
    forcing = forcing.reshape(-1, width)
    forcing = exchange(jnp.broadcast_to(forcing, (modes * ys, *forcing.shape)), (MODE, Y))
    forcing = forcing.reshape(modes, -1, width)
    received = swap_cores(make_history(basis_other, forcing, table, BF16))
    history = make_history(basis, forcing, table, F32)
    return (history + received.astype(F32)).astype(BF16)[None]


def solution(mesh):
    torus = Mesh(mesh.devices.reshape(16, 4, 2, mesh.shape["mode"]), (Z, Y, CORE, MODE))
    bands = (Z, Y, CORE)
    patches = (Z, Y, CORE, MODE)
    in_specs = (P(None, patches, None), P(bands, MODE), P(bands, None, MODE), P(bands), P())
    return jax.shard_map(
        per_device, mesh=torus, in_specs=in_specs, out_specs=P(None, patches, None), check_vma=False
    )
```

time: 119 us -> 117 us (0.983)
  blocking collectives: 54.3 us -> 80.9 us
  starting transfers between devices: 36.2 us -> 23.1 us
  waiting for transfers between devices: 14.9 us -> 1.96 us
  local copies, waits for them, and re-layouts: 3.03 us -> 0.09 us
    all_to_all x4 -> x5, blocking collectives: 54.3 us -> 80.9 us  [exchange(): return lax.all_to_all(value, axis, split_axis=0, concat_axis=0, tiled=True)]
    all_to_all x2 -> x1, waiting for transfers between devices: 13.7 us -> 0.01 us  [exchange(): return lax.all_to_all(value, axis, split_axis=0, concat_axis=0, tiled=True)]
    all_to_all x2 -> x1, starting transfers between devices: 15.8 us -> 4.84 us  [exchange(): return lax.all_to_all(value, axis, split_axis=0, concat_axis=0, tiled=True)]
    unnamed x6 -> x0, local copies, waits for them, and re-layouts: 2.94 us -> none
    ppermute x3, starting transfers between devices: 20.5 us -> 18.2 us  [swap_cores(): return lax.ppermute(value, CORE, [(0, 1), (1, 0)])]
  transfers between devices with their start and end apart: 5 -> 4, of which waited for: 4 -> 2; matrix products, arithmetic and copies ran while one was open for 0% -> 0% of each run, Pallas kernels for 5% -> 6%
where the time goes in v3:
time: 117 us
  blocking collectives  80.9 us (69%)
  starting transfers between devices  23.1 us (20%)
  Pallas kernels  9.12 us (8%)
  waiting for transfers between devices  1.96 us (2%)
    all_to_all x5, blocking collectives, exchange(): return lax.all_to_all(value, axis, split_axis=0, concat_axis=0, tiled=True)  80.9 us
    ppermute x3, starting transfers between devices, swap_cores(): return lax.ppermute(value, CORE, [(0, 1), (1, 0)])  18.2 us
    all_to_all x1, starting transfers between devices, exchange(): return lax.all_to_all(value, axis, split_axis=0, concat_axis=0, tiled=True)  4.84 us
    pallas_call x1, Pallas kernels, make_spectra(): call(functools.partial(sent_kernel, slots, y_count), (spectra, shape((1,...  2.7 us
    pallas_call x1, Pallas kernels, make_spectra(): call(functools.partial(own_kernel, slots, y_count), (table, spectra, shap...  2.47 us
  transfers between devices with their start and end apart: 4, of which 2 were waited for; matrix products, arithmetic and copies ran while one was open for 0% of the time, Pallas kernels for 6%

profile of v3, /device:TPU:1, one launch (start us, length us, event | category | flops | bytes accessed | tf_op | source)
XLA Modules:
  0.0 116.9 jit_solution(4428144274999762005)
XLA Ops:
  0.0 4.8 %all-to-all-start = ((bf16[4,256,256]{2,1,0:T(8,128)(2,1)}), bf16[4,256,256]{2,1,0:T(8,128)(2,1)S(1)}, u32[]{:S(2)}, u32[]{:S(2)}) async-start(bf16[4,256,256]{2,1,0:T(8,128)(2,1)} %bitcast.18), calls=%async_computation | async-start | bytes 1048576 | tf_op jit(solution)/shard_map/all_to_all | solution.py:269
  4.8 0.1 pad_add_fusion.place_ref
  4.9 2.7 %shard_map.55 = (bf16[512,256]{1,0:T(8,128)(2,1)S(1)}, s32[1,512]{1,0:T(1,128)S(1)}, bf16[256,1024]{1,0:T(8,128)(2,1)S(1)}) custom-call(s32[2]{0:T(128)S(1)} %pad_add_fusion.place_ref, s32[1,512]{1,0:T(1,128)} %bitcast.20, bf16[256,1024]{1,0:T(8,128)(2,1)} %bitcast.17), custom_call_target="tpu_custom_call" | custom-call | flops 1 | bytes 1 | tf_op jit(solution)/shard_map/pallas_call | solution.py:132
  7.6 7.4 %collective-permute-start = (bf16[512,256]{1,0:T(8,128)(2,1)S(1)}, bf16[512,256]{1,0:T(8,128)(2,1)S(1)}, u32[]{:S(2)}, u32[]{:S(2)}) collective-permute-start(bf16[512,256]{1,0:T(8,128)(2,1)S(1)} %get-tuple-element.18), channel_id=1, source_target_pairs={{0,4},{4,0},{1,5},{5,1},{2,6},{6,2},{3,7},{7,3},{8,12},{12,8},{9,1... | collective-permute-start | bytes 786440 | tf_op jit(solution)/shard_map/ppermute | solution.py:273
  15.7 2.5 %shard_map.56 = (bf16[512,1024]{1,0:T(8,128)(2,1)S(1)}, bf16[512,256]{1,0:T(8,128)(2,1)S(1)}, bf16[1024,256]{1,0:T(8,128)(2,1)S(1)}, s32[2]{0:T(128)S(1)}) custom-call(s32[2]{0:T(128)S(1)} %pad_add_fusion.place_ref, s32[1]{0:T(128)S(6)} %copy.6.rank_ref, s32[1,512]{1,0:T(1,128)S(1)} %get-tuple-element.15.freq_ref, ...), custom_call_target="tpu_custom_call" | custom-call | flops 1 | bytes 1 | tf_op jit(solution)/shard_map/pallas_call | solution.py:141
  18.2 0.0 collective-permute-done.spectra_ref
  18.2 2.1 %collective-permute-start.1 = (bf16[4,256,256]{2,1,0:T(8,128)(2,1)S(1)}, bf16[4,256,256]{2,1,0:T(8,128)(2,1)S(1)}, u32[]{:S(2)}, u32[]{:S(2)}) collective-permute-start(bf16[4,256,256]{2,1,0:T(8,128)(2,1)S(1)} %all-to-all-done.basis_ref), channel_id=1, source_target_pairs={{0,4},{4,0},{1,5},{5,1},{2,6},{6,2},{3,7},{7,3},{8,12},{12,8},{9,1... | collective-permute-start | bytes 1572872 | tf_op jit(solution)/shard_map/ppermute | solution.py:273
  20.3 0.4 shard_map.57.before_ref
  20.8 1.3 %collective-permute-done.1.basis_ref = bf16[4,256,256]{2,1,0:T(8,128)(2,1)S(1)} collective-permute-done((bf16[4,256,256]{2,1,0:T(8,128)(2,1)S(1)}, bf16[4,256,256]{2,1,0:T(8,128)(2,1)S(1)}, u32[]{:S(2)}, u32[]{:S(2)}) %collective-permute-start.1) | collective-permute-done | bytes 524320 | tf_op jit(solution)/shard_map/ppermute | solution.py:273
  22.0 0.4 shard_map.58
  22.5 20.2 %all_to_all.30.parts_ref = bf16[16,128,256]{2,1,0:T(8,128)(2,1)S(1)} all-to-all(bf16[16,128,256]{2,1,0:T(8,128)(2,1)S(1)} %bitcast.14), channel_id=1, replica_groups=mesh['band_0'=16,'band_1'=4,'band_2'=2,'mode'=4] {'mode','band_1'}, dimensions={0} | all-to-all | bytes 2097152 | tf_op jit(solution)/shard_map/all_to_all | solution.py:269
  42.6 0.1 shard_map.59
  42.8 24.4 %all_to_all.31.parts_ref = bf16[16,8,256]{2,1,0:T(8,128)(2,1)S(1)} all-to-all(bf16[16,8,256]{2,1,0:T(8,128)(2,1)S(1)} %bitcast.15), channel_id=1, replica_groups=mesh['band_0'=16,'band_1'=4,'band_2'=2,'mode'=4] {'band_0'}, dimensions={0} | all-to-all | bytes 131072 | tf_op jit(solution)/shard_map/all_to_all | solution.py:269
  67.2 0.6 shard_map.60
  67.7 6.8 %all_to_all.32.coef_ref = bf16[4,8,256]{2,1,0:T(8,128)(2,1)S(1)} all-to-all(bf16[4,8,256]{2,1,0:T(8,128)(2,1)S(1)} %shard_map.60), channel_id=1, replica_groups=mesh['band_0'=16,'band_1'=4,'band_2'=2,'mode'=4] {'mode'}, dimensions={0} | all-to-all | bytes 32768 | tf_op jit(solution)/shard_map/all_to_all | solution.py:269
  74.6 0.7 shard_map.61
  75.3 14.5 %all_to_all.33 = bf16[16,8,256]{2,1,0:T(8,128)(2,1)S(1)} all-to-all(bf16[16,8,256]{2,1,0:T(8,128)(2,1)S(1)} %shard_map.61), channel_id=1, replica_groups=mesh['band_0'=16,'band_1'=4,'band_2'=2,'mode'=4] {'band_0'}, dimensions={0} | all-to-all | bytes 131072 | tf_op jit(solution)/shard_map/all_to_all | solution.py:269
  89.8 0.1 broadcast_in_dim.6
  89.9 15.0 %all_to_all.34 = bf16[16,128,256]{2,1,0:T(8,128)(2,1)S(1)} all-to-all(bf16[16,128,256]{2,1,0:T(8,128)(2,1)S(1)} %broadcast_in_dim.6), channel_id=1, replica_groups=mesh['band_0'=16,'band_1'=4,'band_2'=2,'mode'=4] {'mode','band_1'}, dimensions={0} | all-to-all | bytes 2097152 | tf_op jit(solution)/shard_map/all_to_all | solution.py:269
  104.9 0.8 shard_map.63
  105.7 8.7 %collective-permute-start.2 = (bf16[256,1024]{1,0:T(8,128)(2,1)S(1)}, bf16[256,1024]{1,0:T(8,128)(2,1)S(1)}, u32[]{:S(2)}, u32[]{:S(2)}) collective-permute-start(bf16[256,1024]{1,0:T(8,128)(2,1)S(1)} %shard_map.63), channel_id=1, source_target_pairs={{0,4},{4,0},{1,5},{5,1},{2,6},{6,2},{3,7},{7,3},{8,12},{12,8},{9,1... | collective-permute-start | bytes 1572872 | tf_op jit(solution)/shard_map/ppermute | solution.py:273
  114.4 0.8 shard_map.62
  115.2 0.7 collective-permute-done.2
  115.9 0.9 fusion
  (1 shorter events, 0.0 us)
Async XLA Ops:
  0.0 18.2 %all-to-all-start = ((bf16[4,256,256]{2,1,0:T(8,128)(2,1)}), bf16[4,256,256]{2,1,0:T(8,128)(2,1)S(1)}, u32[]{:S(2)}, u32[]{:S(2)}) async-start(bf16[4,256,256]{2,1,0:T(8,128)(2,1)} %bitcast.18), calls=%async_computation | async-start | bytes 1048576 | tf_op jit(solution)/shard_map/all_to_all | solution.py:269
  7.6 10.6 %collective-permute-start = (bf16[512,256]{1,0:T(8,128)(2,1)S(1)}, bf16[512,256]{1,0:T(8,128)(2,1)S(1)}, u32[]{:S(2)}, u32[]{:S(2)}) collective-permute-start(bf16[512,256]{1,0:T(8,128)(2,1)S(1)} %get-tuple-element.18), channel_id=1, source_target_pairs={{0,4},{4,0},{1,5},{5,1},{2,6},{6,2},{3,7},{7,3},{8,12},{12,8},{9,1... | collective-permute-start | bytes 786440 | tf_op jit(solution)/shard_map/ppermute | solution.py:273
  18.2 3.8 %collective-permute-start.1 = (bf16[4,256,256]{2,1,0:T(8,128)(2,1)S(1)}, bf16[4,256,256]{2,1,0:T(8,128)(2,1)S(1)}, u32[]{:S(2)}, u32[]{:S(2)}) collective-permute-start(bf16[4,256,256]{2,1,0:T(8,128)(2,1)S(1)} %all-to-all-done.basis_ref), channel_id=1, source_target_pairs={{0,4},{4,0},{1,5},{5,1},{2,6},{6,2},{3,7},{7,3},{8,12},{12,8},{9,1... | collective-permute-start | bytes 1572872 | tf_op jit(solution)/shard_map/ppermute | solution.py:273
  105.7 10.2 %collective-permute-start.2 = (bf16[256,1024]{1,0:T(8,128)(2,1)S(1)}, bf16[256,1024]{1,0:T(8,128)(2,1)S(1)}, u32[]{:S(2)}, u32[]{:S(2)}) collective-permute-start(bf16[256,1024]{1,0:T(8,128)(2,1)S(1)} %shard_map.63), channel_id=1, source_target_pairs={{0,4},{4,0},{1,5},{5,1},{2,6},{6,2},{3,7},{7,3},{8,12},{12,8},{9,1... | collective-permute-start | bytes 1572872 | tf_op jit(solution)/shard_map/ppermute | solution.py:273

commit v4 on v3

--- a/solution.py
+++ b/solution.py
@@ -88,11 +88,13 @@
 
 
 def sent_kernel(
-    slots, y_count, place_ref, freq_ref, velocity_ref, out_ref, freq_in, velocity_in, table, sems
+    slots, y_count, place_ref, freq_ref, velocity_ref, matrix_ref,
+    out_ref, freq_in, velocity_in, matrix_in, table, sems,
 ):
     copies = [
         pltpu.make_async_copy(freq_ref, freq_in, sems.at[0]),
         pltpu.make_async_copy(velocity_ref, velocity_in, sems.at[1]),
+        pltpu.make_async_copy(matrix_ref, matrix_in, sems.at[2]),
     ]
     for copy in copies:
         copy.start()
@@ -100,27 +102,22 @@
     make_table(slots, y_count, 1 - place_ref[0], freq_in, table)
     copies[1].wait()
     out_ref[...] = dot_t(table[...], velocity_in[...]).astype(BF16)
+    copies[2].wait()
 
 
 def own_kernel(
-    slots, y_count, place_ref, rank_ref, freq_ref, velocity_ref, matrix_ref,
-    table_ref, out_ref, rounded_ref, limits_ref, matrix_in, sem,
+    slots, y_count, place_ref, freq_ref, velocity_ref, matrix_ref, table_ref, out_ref, rounded_ref
 ):
-    copy = pltpu.make_async_copy(matrix_ref, matrix_in, sem)
-    copy.start()
-    limits_ref[0] = rank_ref[0]
-    limits_ref[1] = place_ref[1] * matrix_ref.shape[1]
+    rounded_ref[...] = matrix_ref[...].astype(BF16)
     make_table(slots, y_count, place_ref[0], freq_ref, table_ref)
     out_ref[...] = dot_t(table_ref[...], velocity_ref[...]).astype(BF16)
-    copy.wait()
-    rounded_ref[...] = matrix_in[...].astype(BF16)
 
 
 def in_hbm(value):
     return pltpu.with_memory_space_constraint(value, pltpu.HBM)
 
 
-def make_spectra(place, rank, freq_table, velocity, matrix):
+def make_spectra(place, freq_table, velocity, matrix):
     y_count, cores = lax.axis_size(Y), lax.axis_size(CORE)
     all_slots = freq_table.shape[0]
     slots = all_slots // (lax.axis_size(Z) * y_count * cores)
@@ -129,24 +126,28 @@
     rows = 2 * all_slots // cores
     hbm = pl.BlockSpec(memory_space=pltpu.HBM)
     table, spectra = shape((rows, steps), BF16), shape((rows, patches), BF16)
-    sent, freq, velocity = call(
+    sent, freq, velocity, matrix = call(
         functools.partial(sent_kernel, slots, y_count),
-        (spectra, shape((1, all_slots), I32), shape(velocity.shape, BF16)),
+        (
+            spectra,
+            shape((1, all_slots), I32),
+            shape(velocity.shape, BF16),
+            shape(matrix.shape, F32),
+        ),
         1,
         1,
-        in_specs=[SMEM, hbm, hbm],
-        out_specs=(WHOLE, WHOLE, WHOLE),
-        scratch_shapes=[pltpu.VMEM((rows, steps), BF16), pltpu.SemaphoreType.DMA((2,))],
-    )(place, in_hbm(freq_table.reshape(1, -1)), in_hbm(velocity))
+        in_specs=[SMEM, hbm, hbm, hbm],
+        out_specs=(WHOLE, WHOLE, WHOLE, WHOLE),
+        scratch_shapes=[pltpu.VMEM((rows, steps), BF16), pltpu.SemaphoreType.DMA((3,))],
+    )(place, in_hbm(freq_table.reshape(1, -1)), in_hbm(velocity), in_hbm(matrix))
     own = call(
         functools.partial(own_kernel, slots, y_count),
-        (table, spectra, shape(matrix.shape, BF16), shape((2,), I32)),
+        (table, spectra, shape(matrix.shape, BF16)),
         1,
         1,
-        in_specs=[SMEM, SMEM, WHOLE, WHOLE, hbm],
-        out_specs=(WHOLE, WHOLE, WHOLE, SMEM),
-        scratch_shapes=[pltpu.VMEM(matrix.shape, F32), pltpu.SemaphoreType.DMA],
-    )(place, rank, freq, velocity, in_hbm(matrix))
+        in_specs=[SMEM, WHOLE, WHOLE, WHOLE],
+        out_specs=(WHOLE, WHOLE, WHOLE),
+    )(place, freq, velocity, matrix)
     return sent, *own
 
 
@@ -199,44 +200,44 @@
     )(parts)
 
 
-def kept(value, limits_ref):
-    index = lax.broadcasted_iota(I32, value.shape, 1) + limits_ref[1]
-    return jnp.where(index < limits_ref[0], value, 0.0)
-
-
-def coefficients_kernel(limits_ref, parts_ref, out_ref):
-    value = kept(added(parts_ref), limits_ref).astype(BF16)
+def kept(value, limit_ref):
+    index = lax.broadcasted_iota(I32, value.shape, 1)
+    return jnp.where(index < limit_ref[:1, :1], value, 0.0)
+
+
+def coefficients_kernel(limit_ref, parts_ref, out_ref):
+    value = kept(added(parts_ref), limit_ref).astype(BF16)
     out_ref[...] = jnp.broadcast_to(value, out_ref.shape)
 
 
-def make_coefficients(limits, parts, copies):
+def make_coefficients(limit, parts, copies):
     return call(
         coefficients_kernel,
         shape((copies, *parts.shape[1:]), BF16),
         parts.size,
-        in_specs=[SMEM, WHOLE],
+        in_specs=[WHOLE, WHOLE],
         out_specs=WHOLE,
-    )(limits, parts)
-
-
-def forcing_kernel(limits_ref, coef_ref, matrix_ref, out_ref):
+    )(limit, parts)
+
+
+def forcing_kernel(limit_ref, coef_ref, matrix_ref, out_ref):
     width = coef_ref.shape[2]
     total = dot(coef_ref[0], matrix_ref[:width])
     for k in range(1, coef_ref.shape[0]):
         total = total + dot(coef_ref[k], matrix_ref[k * width : (k + 1) * width])
-    value = kept(2.0 * total, limits_ref).astype(BF16)
+    value = kept(2.0 * total, limit_ref).astype(BF16)
     out_ref[...] = jnp.broadcast_to(value, out_ref.shape)
 
 
-def make_forcing(limits, coef, matrix, copies):
+def make_forcing(limit, coef, matrix, copies):
     rows = coef.shape[1]
     return call(
         forcing_kernel,
         shape((copies, rows, matrix.shape[1]), BF16),
         2 * rows * matrix.size,
-        in_specs=[SMEM, WHOLE, WHOLE],
+        in_specs=[WHOLE, WHOLE, WHOLE],
         out_specs=WHOLE,
-    )(limits, coef, matrix)
+    )(limit, coef, matrix)
 
 
 def history_kernel(basis_ref, forcing_ref, table_ref, *rest):
@@ -276,20 +277,21 @@
 def per_device(velocity, radiation_modes, resistance, mode_ranks, freq_table):
     modes, ys, zs = lax.axis_size(MODE), lax.axis_size(Y), lax.axis_size(Z)
     width = radiation_modes.shape[1]
-    place = jnp.stack([lax.axis_index(CORE), lax.axis_index(MODE)])
+    place = lax.axis_index(CORE).reshape(1)
     basis = exchange(radiation_modes.reshape(modes, -1, width), MODE)
-    sent, table, spectra, matrix, limits = make_spectra(
-        place, mode_ranks, freq_table, velocity[0], resistance[0]
+    sent, table, spectra, matrix = make_spectra(place, freq_table, velocity[0], resistance[0])
+    spectra_other = swap_cores(sent)
+    limit = jnp.broadcast_to(mode_ranks[0] - lax.axis_index(MODE) * width, (8, LANES))
+    basis, spectra, spectra_other, limit = lax.optimization_barrier(
+        (basis, spectra, spectra_other, limit)
     )
-    spectra_other = swap_cores(sent)
-    basis, spectra, spectra_other = lax.optimization_barrier((basis, spectra, spectra_other))
     basis_other = swap_cores(basis)
     coef = first_partial(spectra, basis)
     coef = make_partial(spectra_other, basis_other, coef)
     coef = summed(exchange(coef.reshape(modes * ys, -1, width), (MODE, Y)))
     coef = exchange(coef.reshape(zs, -1, width), Z)
-    coef = exchange(make_coefficients(limits, coef, modes), MODE)
-    forcing = exchange(make_forcing(limits, coef, matrix, zs), Z)
+    coef = exchange(make_coefficients(limit, coef, modes), MODE)
+    forcing = exchange(make_forcing(limit, coef, matrix, zs), Z)
     forcing = forcing.reshape(-1, width)
     forcing = exchange(jnp.broadcast_to(forcing, (modes * ys, *forcing.shape)), (MODE, Y))
     forcing = forcing.reshape(modes, -1, width)

time: 117 us -> 115 us (0.983)
  Pallas kernels: 9.12 us -> 6.42 us
  starting transfers between devices: 23.1 us -> 25.1 us
  blocking collectives: 80.9 us -> 79.7 us
    ppermute x3, starting transfers between devices: 18.2 us -> 20.2 us  [swap_cores(): return lax.ppermute(value, CORE, [(0, 1), (1, 0)])]
    all_to_all x5, blocking collectives: 80.9 us -> 79.7 us  [exchange(): return lax.all_to_all(value, axis, split_axis=0, concat_axis=0, tiled=True)]
  transfers between devices with their start and end apart: 4 -> 4, of which waited for: 2 -> 2; matrix products, arithmetic and copies ran while one was open for 0% -> 0% of each run, Pallas kernels for 6% -> 4%
where the time goes in v4:
time: 115 us
  blocking collectives  79.7 us (69%)
  starting transfers between devices  25.1 us (22%)
  Pallas kernels  6.42 us (6%)
  waiting for transfers between devices  1.77 us (2%)
    all_to_all x5, blocking collectives, exchange(): return lax.all_to_all(value, axis, split_axis=0, concat_axis=0, tiled=True)  79.7 us
    ppermute x3, starting transfers between devices, swap_cores(): return lax.ppermute(value, CORE, [(0, 1), (1, 0)])  20.2 us
    all_to_all x1, starting transfers between devices, exchange(): return lax.all_to_all(value, axis, split_axis=0, concat_axis=0, tiled=True)  4.84 us
  transfers between devices with their start and end apart: 4, of which 2 were waited for; matrix products, arithmetic and copies ran while one was open for 0% of the time, Pallas kernels for 4%

profile of v4, /device:TPU:1, one launch (start us, length us, event | category | flops | bytes accessed | tf_op | source)
XLA Modules:
  0.0 114.7 jit_solution(2142709887201235727)
XLA Ops:
  0.0 4.8 %all-to-all-start = ((bf16[4,256,256]{2,1,0:T(8,128)(2,1)}), bf16[4,256,256]{2,1,0:T(8,128)(2,1)S(1)}, u32[]{:S(2)}, u32[]{:S(2)}) async-start(bf16[4,256,256]{2,1,0:T(8,128)(2,1)} %bitcast.19), calls=%async_computation | async-start | bytes 1048576 | tf_op jit(solution)/shard_map/all_to_all | solution.py:270
  4.8 2.2 %shard_map.55 = (bf16[512,256]{1,0:T(8,128)(2,1)S(1)}, s32[1,512]{1,0:T(1,128)S(1)}, bf16[256,1024]{1,0:T(8,128)(2,1)S(1)}, f32[1024,256]{1,0:T(8,128)S(1)}) custom-call(s32[1]{0:T(128)} %bitcast.1.place_ref, s32[1,512]{1,0:T(1,128)} %bitcast.21, bf16[256,1024]{1,0:T(8,128)(2,1)} %bitcast.18, f32[1024,256]{1,0:T(8,128)} %bitcast.17), custom_call_target="tpu_custom_call" | custom-call | flops 1 | bytes 1 | tf_op jit(solution)/shard_map/pallas_call | solution.py:129
  7.0 7.4 %collective-permute-start = (bf16[512,256]{1,0:T(8,128)(2,1)S(1)}, bf16[512,256]{1,0:T(8,128)(2,1)S(1)}, u32[]{:S(2)}, u32[]{:S(2)}) collective-permute-start(bf16[512,256]{1,0:T(8,128)(2,1)S(1)} %get-tuple-element.20), channel_id=1, source_target_pairs={{0,4},{4,0},{1,5},{5,1},{2,6},{6,2},{3,7},{7,3},{8,12},{12,8},{9,1... | collective-permute-start | bytes 786440 | tf_op jit(solution)/shard_map/ppermute | solution.py:274
  14.5 1.4 %shard_map.56 = (bf16[512,1024]{1,0:T(8,128)(2,1)S(1)}, bf16[512,256]{1,0:T(8,128)(2,1)S(1)}, bf16[1024,256]{1,0:T(8,128)(2,1)S(1)}) custom-call(s32[1]{0:T(128)} %bitcast.1.place_ref, s32[1,512]{1,0:T(1,128)S(1)} %get-tuple-element.16.freq_ref, bf16[256,1024]{1,0:T(8,128)(2,1)S(1)} %get-tuple-element.17.velocity_ref, ...), custom_call_target="tpu_custom_call" | custom-call | flops 1 | bytes 1 | tf_op jit(solution)/shard_map/pallas_call | solution.py:143
  16.5 0.0 collective-permute-done.spectra_ref
  16.5 0.0 all-to-all-done.basis_ref
  16.5 3.8 %collective-permute-start.1 = (bf16[4,256,256]{2,1,0:T(8,128)(2,1)S(1)}, bf16[4,256,256]{2,1,0:T(8,128)(2,1)S(1)}, u32[]{:S(2)}, u32[]{:S(2)}) collective-permute-start(bf16[4,256,256]{2,1,0:T(8,128)(2,1)S(1)} %all-to-all-done.basis_ref), channel_id=1, source_target_pairs={{0,4},{4,0},{1,5},{5,1},{2,6},{6,2},{3,7},{7,3},{8,12},{12,8},{9,1... | collective-permute-start | bytes 1572872 | tf_op jit(solution)/shard_map/ppermute | solution.py:274
  20.3 0.4 shard_map.57.before_ref
  20.8 1.1 collective-permute-done.1.basis_ref
  21.8 0.4 shard_map.58
  22.3 18.7 %all_to_all.30.parts_ref = bf16[16,128,256]{2,1,0:T(8,128)(2,1)S(1)} all-to-all(bf16[16,128,256]{2,1,0:T(8,128)(2,1)S(1)} %bitcast.15), channel_id=1, replica_groups=mesh['band_0'=16,'band_1'=4,'band_2'=2,'mode'=4] {'mode','band_1'}, dimensions={0} | all-to-all | bytes 2097152 | tf_op jit(solution)/shard_map/all_to_all | solution.py:270
  40.9 0.1 shard_map.59
  41.1 25.3 %all_to_all.31.parts_ref = bf16[16,8,256]{2,1,0:T(8,128)(2,1)S(1)} all-to-all(bf16[16,8,256]{2,1,0:T(8,128)(2,1)S(1)} %bitcast.16), channel_id=1, replica_groups=mesh['band_0'=16,'band_1'=4,'band_2'=2,'mode'=4] {'band_0'}, dimensions={0} | all-to-all | bytes 131072 | tf_op jit(solution)/shard_map/all_to_all | solution.py:270
  66.4 6.6 %all_to_all.32.coef_ref = bf16[4,8,256]{2,1,0:T(8,128)(2,1)S(1)} all-to-all(bf16[4,8,256]{2,1,0:T(8,128)(2,1)S(1)} %shard_map.60), channel_id=1, replica_groups=mesh['band_0'=16,'band_1'=4,'band_2'=2,'mode'=4] {'mode'}, dimensions={0} | all-to-all | bytes 32768 | tf_op jit(solution)/shard_map/all_to_all | solution.py:270
  73.0 0.2 shard_map.61
  73.1 14.3 %all_to_all.33 = bf16[16,8,256]{2,1,0:T(8,128)(2,1)S(1)} all-to-all(bf16[16,8,256]{2,1,0:T(8,128)(2,1)S(1)} %shard_map.61), channel_id=1, replica_groups=mesh['band_0'=16,'band_1'=4,'band_2'=2,'mode'=4] {'band_0'}, dimensions={0} | all-to-all | bytes 131072 | tf_op jit(solution)/shard_map/all_to_all | solution.py:270
  87.4 0.1 broadcast_in_dim.10
  87.5 14.9 %all_to_all.34 = bf16[16,128,256]{2,1,0:T(8,128)(2,1)S(1)} all-to-all(bf16[16,128,256]{2,1,0:T(8,128)(2,1)S(1)} %broadcast_in_dim.10), channel_id=1, replica_groups=mesh['band_0'=16,'band_1'=4,'band_2'=2,'mode'=4] {'mode','band_1'}, dimensions={0} | all-to-all | bytes 2097152 | tf_op jit(solution)/shard_map/all_to_all | solution.py:270
  102.5 0.8 shard_map.63
  103.3 9.0 %collective-permute-start.2 = (bf16[256,1024]{1,0:T(8,128)(2,1)S(1)}, bf16[256,1024]{1,0:T(8,128)(2,1)S(1)}, u32[]{:S(2)}, u32[]{:S(2)}) collective-permute-start(bf16[256,1024]{1,0:T(8,128)(2,1)S(1)} %shard_map.63), channel_id=1, source_target_pairs={{0,4},{4,0},{1,5},{5,1},{2,6},{6,2},{3,7},{7,3},{8,12},{12,8},{9,1... | collective-permute-start | bytes 1572872 | tf_op jit(solution)/shard_map/ppermute | solution.py:274
  112.3 0.8 shard_map.62
  113.1 0.7 collective-permute-done.2
  113.8 0.9 fusion
  (2 shorter events, 0.0 us)
Async XLA Ops:
  0.0 16.5 %all-to-all-start = ((bf16[4,256,256]{2,1,0:T(8,128)(2,1)}), bf16[4,256,256]{2,1,0:T(8,128)(2,1)S(1)}, u32[]{:S(2)}, u32[]{:S(2)}) async-start(bf16[4,256,256]{2,1,0:T(8,128)(2,1)} %bitcast.19), calls=%async_computation | async-start | bytes 1048576 | tf_op jit(solution)/shard_map/all_to_all | solution.py:270
  7.0 9.5 %collective-permute-start = (bf16[512,256]{1,0:T(8,128)(2,1)S(1)}, bf16[512,256]{1,0:T(8,128)(2,1)S(1)}, u32[]{:S(2)}, u32[]{:S(2)}) collective-permute-start(bf16[512,256]{1,0:T(8,128)(2,1)S(1)} %get-tuple-element.20), channel_id=1, source_target_pairs={{0,4},{4,0},{1,5},{5,1},{2,6},{6,2},{3,7},{7,3},{8,12},{12,8},{9,1... | collective-permute-start | bytes 786440 | tf_op jit(solution)/shard_map/ppermute | solution.py:274
  16.5 5.3 %collective-permute-start.1 = (bf16[4,256,256]{2,1,0:T(8,128)(2,1)S(1)}, bf16[4,256,256]{2,1,0:T(8,128)(2,1)S(1)}, u32[]{:S(2)}, u32[]{:S(2)}) collective-permute-start(bf16[4,256,256]{2,1,0:T(8,128)(2,1)S(1)} %all-to-all-done.basis_ref), channel_id=1, source_target_pairs={{0,4},{4,0},{1,5},{5,1},{2,6},{6,2},{3,7},{7,3},{8,12},{12,8},{9,1... | collective-permute-start | bytes 1572872 | tf_op jit(solution)/shard_map/ppermute | solution.py:274
  103.3 10.5 %collective-permute-start.2 = (bf16[256,1024]{1,0:T(8,128)(2,1)S(1)}, bf16[256,1024]{1,0:T(8,128)(2,1)S(1)}, u32[]{:S(2)}, u32[]{:S(2)}) collective-permute-start(bf16[256,1024]{1,0:T(8,128)(2,1)S(1)} %shard_map.63), channel_id=1, source_target_pairs={{0,4},{4,0},{1,5},{5,1},{2,6},{6,2},{3,7},{7,3},{8,12},{12,8},{9,1... | collective-permute-start | bytes 1572872 | tf_op jit(solution)/shard_map/ppermute | solution.py:274

commit v5 on v4

--- a/solution.py
+++ b/solution.py
@@ -256,14 +256,33 @@
         history_kernel,
         shape((patches, steps), dtype),
         2 * rows * patches * (steps + parts * width),
-        grid=(1,),
-        in_specs=[
-            pl.BlockSpec(basis.shape, lambda i: (0, 0, 0)),
-            pl.BlockSpec(forcing.shape, lambda i: (0, 0, 0)),
-            pl.BlockSpec((rows, steps), lambda i: (0, 0)),
-        ],
-        out_specs=pl.BlockSpec((patches, steps), lambda i: (0, 0)),
+        in_specs=[WHOLE, WHOLE, WHOLE],
+        out_specs=WHOLE,
     )(basis, forcing, table)
+
+
+def finish_kernel(own_ref, received_ref, out_ref, done, sems):
+    pieces = sems.shape[0]
+    rows = own_ref.shape[0] // pieces
+    copies = []
+    for k in range(pieces):
+        here = pl.ds(k * rows, rows)
+        done[here] = (own_ref[here] + received_ref[here].astype(F32)).astype(BF16)
+        copies.append(pltpu.make_async_copy(done.at[here], out_ref.at[here], sems.at[k]))
+        copies[-1].start()
+    for copy in copies:
+        copy.wait()
+
+
+def finish(own, received):
+    return call(
+        finish_kernel,
+        shape(own.shape, BF16),
+        own.size,
+        in_specs=[WHOLE, WHOLE],
+        out_specs=pl.BlockSpec(memory_space=pltpu.HBM),
+        scratch_shapes=[pltpu.VMEM(own.shape, BF16), pltpu.SemaphoreType.DMA((4,))],
+    )(own, received)
 
 
 def exchange(value, axis):
@@ -297,7 +316,7 @@
     forcing = forcing.reshape(modes, -1, width)
     received = swap_cores(make_history(basis_other, forcing, table, BF16))
     history = make_history(basis, forcing, table, F32)
-    return (history + received.astype(F32)).astype(BF16)[None]
+    return finish(history, received)[None]
 
 
 def solution(mesh):

time: 115 us -> 115 us (level)
  no operation moved by 1% of the time
where the time goes in v5:
time: 115 us
  blocking collectives  79.7 us (69%)
  starting transfers between devices  25.1 us (22%)
  Pallas kernels  7.26 us (6%)
  waiting for transfers between devices  1.77 us (2%)
    all_to_all x5, blocking collectives, exchange(): return lax.all_to_all(value, axis, split_axis=0, concat_axis=0, tiled=True)  79.7 us
    ppermute x3, starting transfers between devices, swap_cores(): return lax.ppermute(value, CORE, [(0, 1), (1, 0)])  20.2 us
    all_to_all x1, starting transfers between devices, exchange(): return lax.all_to_all(value, axis, split_axis=0, concat_axis=0, tiled=True)  4.84 us
  transfers between devices with their start and end apart: 4, of which 2 were waited for; matrix products, arithmetic and copies ran while one was open for 0% of the time, Pallas kernels for 4%

profile of v5, /device:TPU:1, one launch (start us, length us, event | category | flops | bytes accessed | tf_op | source)
XLA Modules:
  0.0 114.7 jit_solution(9969775547174989376)
XLA Ops:
  0.0 4.8 %all-to-all-start = ((bf16[4,256,256]{2,1,0:T(8,128)(2,1)}), bf16[4,256,256]{2,1,0:T(8,128)(2,1)S(1)}, u32[]{:S(2)}, u32[]{:S(2)}) async-start(bf16[4,256,256]{2,1,0:T(8,128)(2,1)} %bitcast.18), calls=%async_computation | async-start | bytes 1048576 | tf_op jit(solution)/shard_map/all_to_all | solution.py:289
  4.8 2.2 %shard_map.55 = (bf16[512,256]{1,0:T(8,128)(2,1)S(1)}, s32[1,512]{1,0:T(1,128)S(1)}, bf16[256,1024]{1,0:T(8,128)(2,1)S(1)}, f32[1024,256]{1,0:T(8,128)S(1)}) custom-call(s32[1]{0:T(128)} %bitcast.1.place_ref, s32[1,512]{1,0:T(1,128)} %bitcast.20, bf16[256,1024]{1,0:T(8,128)(2,1)} %bitcast.17, f32[1024,256]{1,0:T(8,128)} %bitcast.16), custom_call_target="tpu_custom_call" | custom-call | flops 1 | bytes 1 | tf_op jit(solution)/shard_map/pallas_call | solution.py:129
  7.0 7.4 %collective-permute-start = (bf16[512,256]{1,0:T(8,128)(2,1)S(1)}, bf16[512,256]{1,0:T(8,128)(2,1)S(1)}, u32[]{:S(2)}, u32[]{:S(2)}) collective-permute-start(bf16[512,256]{1,0:T(8,128)(2,1)S(1)} %get-tuple-element.20), channel_id=1, source_target_pairs={{0,4},{4,0},{1,5},{5,1},{2,6},{6,2},{3,7},{7,3},{8,12},{12,8},{9,1... | collective-permute-start | bytes 786440 | tf_op jit(solution)/shard_map/ppermute | solution.py:293
  14.5 1.4 %shard_map.56 = (bf16[512,1024]{1,0:T(8,128)(2,1)S(1)}, bf16[512,256]{1,0:T(8,128)(2,1)S(1)}, bf16[1024,256]{1,0:T(8,128)(2,1)S(1)}) custom-call(s32[1]{0:T(128)} %bitcast.1.place_ref, s32[1,512]{1,0:T(1,128)S(1)} %get-tuple-element.16.freq_ref, bf16[256,1024]{1,0:T(8,128)(2,1)S(1)} %get-tuple-element.17.velocity_ref, ...), custom_call_target="tpu_custom_call" | custom-call | flops 1 | bytes 1 | tf_op jit(solution)/shard_map/pallas_call | solution.py:143
  16.5 0.0 collective-permute-done.spectra_ref
  16.5 0.0 all-to-all-done.basis_ref
  16.5 3.8 %collective-permute-start.1 = (bf16[4,256,256]{2,1,0:T(8,128)(2,1)S(1)}, bf16[4,256,256]{2,1,0:T(8,128)(2,1)S(1)}, u32[]{:S(2)}, u32[]{:S(2)}) collective-permute-start(bf16[4,256,256]{2,1,0:T(8,128)(2,1)S(1)} %all-to-all-done.basis_ref), channel_id=1, source_target_pairs={{0,4},{4,0},{1,5},{5,1},{2,6},{6,2},{3,7},{7,3},{8,12},{12,8},{9,1... | collective-permute-start | bytes 1572872 | tf_op jit(solution)/shard_map/ppermute | solution.py:293
  20.3 0.4 shard_map.57.before_ref
  20.8 1.1 collective-permute-done.1.basis_ref
  21.8 0.4 shard_map.58
  22.3 18.7 %all_to_all.30.parts_ref = bf16[16,128,256]{2,1,0:T(8,128)(2,1)S(1)} all-to-all(bf16[16,128,256]{2,1,0:T(8,128)(2,1)S(1)} %bitcast.14), channel_id=1, replica_groups=mesh['band_0'=16,'band_1'=4,'band_2'=2,'mode'=4] {'mode','band_1'}, dimensions={0} | all-to-all | bytes 2097152 | tf_op jit(solution)/shard_map/all_to_all | solution.py:289
  40.9 0.1 shard_map.59
  41.1 25.3 %all_to_all.31.parts_ref = bf16[16,8,256]{2,1,0:T(8,128)(2,1)S(1)} all-to-all(bf16[16,8,256]{2,1,0:T(8,128)(2,1)S(1)} %bitcast.15), channel_id=1, replica_groups=mesh['band_0'=16,'band_1'=4,'band_2'=2,'mode'=4] {'band_0'}, dimensions={0} | all-to-all | bytes 131072 | tf_op jit(solution)/shard_map/all_to_all | solution.py:289
  66.4 6.6 %all_to_all.32.coef_ref = bf16[4,8,256]{2,1,0:T(8,128)(2,1)S(1)} all-to-all(bf16[4,8,256]{2,1,0:T(8,128)(2,1)S(1)} %shard_map.60), channel_id=1, replica_groups=mesh['band_0'=16,'band_1'=4,'band_2'=2,'mode'=4] {'mode'}, dimensions={0} | all-to-all | bytes 32768 | tf_op jit(solution)/shard_map/all_to_all | solution.py:289
  73.0 0.2 shard_map.61
  73.1 14.3 %all_to_all.33 = bf16[16,8,256]{2,1,0:T(8,128)(2,1)S(1)} all-to-all(bf16[16,8,256]{2,1,0:T(8,128)(2,1)S(1)} %shard_map.61), channel_id=1, replica_groups=mesh['band_0'=16,'band_1'=4,'band_2'=2,'mode'=4] {'band_0'}, dimensions={0} | all-to-all | bytes 131072 | tf_op jit(solution)/shard_map/all_to_all | solution.py:289
  87.4 0.1 broadcast_in_dim.10
  87.5 14.9 %all_to_all.34 = bf16[16,128,256]{2,1,0:T(8,128)(2,1)S(1)} all-to-all(bf16[16,128,256]{2,1,0:T(8,128)(2,1)S(1)} %broadcast_in_dim.10), channel_id=1, replica_groups=mesh['band_0'=16,'band_1'=4,'band_2'=2,'mode'=4] {'mode','band_1'}, dimensions={0} | all-to-all | bytes 2097152 | tf_op jit(solution)/shard_map/all_to_all | solution.py:289
  102.5 0.8 shard_map.63
  103.3 9.0 %collective-permute-start.2 = (bf16[256,1024]{1,0:T(8,128)(2,1)S(1)}, bf16[256,1024]{1,0:T(8,128)(2,1)S(1)}, u32[]{:S(2)}, u32[]{:S(2)}) collective-permute-start(bf16[256,1024]{1,0:T(8,128)(2,1)S(1)} %shard_map.63), channel_id=1, source_target_pairs={{0,4},{4,0},{1,5},{5,1},{2,6},{6,2},{3,7},{7,3},{8,12},{12,8},{9,1... | collective-permute-start | bytes 1572872 | tf_op jit(solution)/shard_map/ppermute | solution.py:293
  112.3 0.8 shard_map.62.own_ref
  113.1 0.7 collective-permute-done.2.received_ref
  113.8 0.8 shard_map.64
  (2 shorter events, 0.0 us)
Async XLA Ops:
  0.0 16.5 %all-to-all-start = ((bf16[4,256,256]{2,1,0:T(8,128)(2,1)}), bf16[4,256,256]{2,1,0:T(8,128)(2,1)S(1)}, u32[]{:S(2)}, u32[]{:S(2)}) async-start(bf16[4,256,256]{2,1,0:T(8,128)(2,1)} %bitcast.18), calls=%async_computation | async-start | bytes 1048576 | tf_op jit(solution)/shard_map/all_to_all | solution.py:289
  7.0 9.5 %collective-permute-start = (bf16[512,256]{1,0:T(8,128)(2,1)S(1)}, bf16[512,256]{1,0:T(8,128)(2,1)S(1)}, u32[]{:S(2)}, u32[]{:S(2)}) collective-permute-start(bf16[512,256]{1,0:T(8,128)(2,1)S(1)} %get-tuple-element.20), channel_id=1, source_target_pairs={{0,4},{4,0},{1,5},{5,1},{2,6},{6,2},{3,7},{7,3},{8,12},{12,8},{9,1... | collective-permute-start | bytes 786440 | tf_op jit(solution)/shard_map/ppermute | solution.py:293
  16.5 5.3 %collective-permute-start.1 = (bf16[4,256,256]{2,1,0:T(8,128)(2,1)S(1)}, bf16[4,256,256]{2,1,0:T(8,128)(2,1)S(1)}, u32[]{:S(2)}, u32[]{:S(2)}) collective-permute-start(bf16[4,256,256]{2,1,0:T(8,128)(2,1)S(1)} %all-to-all-done.basis_ref), channel_id=1, source_target_pairs={{0,4},{4,0},{1,5},{5,1},{2,6},{6,2},{3,7},{7,3},{8,12},{12,8},{9,1... | collective-permute-start | bytes 1572872 | tf_op jit(solution)/shard_map/ppermute | solution.py:293
  103.3 10.5 %collective-permute-start.2 = (bf16[256,1024]{1,0:T(8,128)(2,1)S(1)}, bf16[256,1024]{1,0:T(8,128)(2,1)S(1)}, u32[]{:S(2)}, u32[]{:S(2)}) collective-permute-start(bf16[256,1024]{1,0:T(8,128)(2,1)S(1)} %shard_map.63), channel_id=1, source_target_pairs={{0,4},{4,0},{1,5},{5,1},{2,6},{6,2},{3,7},{7,3},{8,12},{12,8},{9,1... | collective-permute-start | bytes 1572872 | tf_op jit(solution)/shard_map/ppermute | solution.py:293

commit v6 on v4

--- a/solution.py
+++ b/solution.py
@@ -13,7 +13,6 @@
 F32, BF16, I32 = jnp.float32, jnp.bfloat16, jnp.int32
 LANES = 128
 VMEM_BYTES = 24 * 1024 * 1024
-SMEM = pl.BlockSpec(memory_space=pltpu.SMEM)
 WHOLE = pl.BlockSpec(memory_space=pltpu.VMEM)
 
 
@@ -88,7 +87,7 @@
 
 
 def sent_kernel(
-    slots, y_count, place_ref, freq_ref, velocity_ref, matrix_ref,
+    slots, y_count, freq_ref, velocity_ref, matrix_ref,
     out_ref, freq_in, velocity_in, matrix_in, table, sems,
 ):
     copies = [
@@ -99,17 +98,17 @@
     for copy in copies:
         copy.start()
     copies[0].wait()
-    make_table(slots, y_count, 1 - place_ref[0], freq_in, table)
+    make_table(slots, y_count, 1 - lax.axis_index(CORE), freq_in, table)
     copies[1].wait()
     out_ref[...] = dot_t(table[...], velocity_in[...]).astype(BF16)
     copies[2].wait()
 
 
 def own_kernel(
-    slots, y_count, place_ref, freq_ref, velocity_ref, matrix_ref, table_ref, out_ref, rounded_ref
+    slots, y_count, freq_ref, velocity_ref, matrix_ref, table_ref, out_ref, rounded_ref
 ):
     rounded_ref[...] = matrix_ref[...].astype(BF16)
-    make_table(slots, y_count, place_ref[0], freq_ref, table_ref)
+    make_table(slots, y_count, lax.axis_index(CORE), freq_ref, table_ref)
     out_ref[...] = dot_t(table_ref[...], velocity_ref[...]).astype(BF16)
 
 
@@ -117,7 +116,7 @@
     return pltpu.with_memory_space_constraint(value, pltpu.HBM)
 
 
-def make_spectra(place, freq_table, velocity, matrix):
+def make_spectra(freq_table, velocity, matrix):
     y_count, cores = lax.axis_size(Y), lax.axis_size(CORE)
     all_slots = freq_table.shape[0]
     slots = all_slots // (lax.axis_size(Z) * y_count * cores)
@@ -136,18 +135,18 @@
         ),
         1,
         1,
-        in_specs=[SMEM, hbm, hbm, hbm],
+        in_specs=[hbm, hbm, hbm],
         out_specs=(WHOLE, WHOLE, WHOLE, WHOLE),
         scratch_shapes=[pltpu.VMEM((rows, steps), BF16), pltpu.SemaphoreType.DMA((3,))],
-    )(place, in_hbm(freq_table.reshape(1, -1)), in_hbm(velocity), in_hbm(matrix))
+    )(in_hbm(freq_table.reshape(1, -1)), in_hbm(velocity), in_hbm(matrix))
     own = call(
         functools.partial(own_kernel, slots, y_count),
         (table, spectra, shape(matrix.shape, BF16)),
         1,
         1,
-        in_specs=[SMEM, WHOLE, WHOLE, WHOLE],
+        in_specs=[WHOLE, WHOLE, WHOLE],
         out_specs=(WHOLE, WHOLE, WHOLE),
-    )(place, freq, velocity, matrix)
+    )(freq, velocity, matrix)
     return sent, *own
 
 
@@ -277,9 +276,8 @@
 def per_device(velocity, radiation_modes, resistance, mode_ranks, freq_table):
     modes, ys, zs = lax.axis_size(MODE), lax.axis_size(Y), lax.axis_size(Z)
     width = radiation_modes.shape[1]
-    place = lax.axis_index(CORE).reshape(1)
     basis = exchange(radiation_modes.reshape(modes, -1, width), MODE)
-    sent, table, spectra, matrix = make_spectra(place, freq_table, velocity[0], resistance[0])
+    sent, table, spectra, matrix = make_spectra(freq_table, velocity[0], resistance[0])
     spectra_other = swap_cores(sent)
     limit = jnp.broadcast_to(mode_ranks[0] - lax.axis_index(MODE) * width, (8, LANES))
     basis, spectra, spectra_other, limit = lax.optimization_barrier(

time: 115 us -> 115 us (level)
  no operation moved by 1% of the time
where the time goes in v6:
time: 115 us
  blocking collectives  79.7 us (69%)
  starting transfers between devices  25.1 us (22%)
  Pallas kernels  6.42 us (6%)
  waiting for transfers between devices  1.77 us (2%)
    all_to_all x5, blocking collectives, exchange(): return lax.all_to_all(value, axis, split_axis=0, concat_axis=0, tiled=True)  79.7 us
    ppermute x3, starting transfers between devices, swap_cores(): return lax.ppermute(value, CORE, [(0, 1), (1, 0)])  20.2 us
    all_to_all x1, starting transfers between devices, exchange(): return lax.all_to_all(value, axis, split_axis=0, concat_axis=0, tiled=True)  4.84 us
  transfers between devices with their start and end apart: 4, of which 2 were waited for; matrix products, arithmetic and copies ran while one was open for 0% of the time, Pallas kernels for 4%

profile of v6, /device:TPU:1, one launch (start us, length us, event | category | flops | bytes accessed | tf_op | source)
XLA Modules:
  0.0 114.7 jit_solution(3827655445993000873)
XLA Ops:
  0.0 4.8 %all-to-all-start = ((bf16[4,256,256]{2,1,0:T(8,128)(2,1)}), bf16[4,256,256]{2,1,0:T(8,128)(2,1)S(1)}, u32[]{:S(2)}, u32[]{:S(2)}) async-start(bf16[4,256,256]{2,1,0:T(8,128)(2,1)} %bitcast.18), calls=%async_computation | async-start | bytes 1048576 | tf_op jit(solution)/shard_map/all_to_all | solution.py:269
  4.8 2.2 %shard_map.55 = (bf16[512,256]{1,0:T(8,128)(2,1)S(1)}, s32[1,512]{1,0:T(1,128)S(1)}, bf16[256,1024]{1,0:T(8,128)(2,1)S(1)}, f32[1024,256]{1,0:T(8,128)S(1)}) custom-call(s32[1,512]{1,0:T(1,128)} %bitcast.20, bf16[256,1024]{1,0:T(8,128)(2,1)} %bitcast.17, f32[1024,256]{1,0:T(8,128)} %bitcast.16), custom_call_target="tpu_custom_call" | custom-call | flops 1 | bytes 1 | tf_op jit(solution)/shard_map/pallas_call | solution.py:128
  7.0 7.4 %collective-permute-start = (bf16[512,256]{1,0:T(8,128)(2,1)S(1)}, bf16[512,256]{1,0:T(8,128)(2,1)S(1)}, u32[]{:S(2)}, u32[]{:S(2)}) collective-permute-start(bf16[512,256]{1,0:T(8,128)(2,1)S(1)} %get-tuple-element.20), channel_id=1, source_target_pairs={{0,4},{4,0},{1,5},{5,1},{2,6},{6,2},{3,7},{7,3},{8,12},{12,8},{9,1... | collective-permute-start | bytes 786440 | tf_op jit(solution)/shard_map/ppermute | solution.py:273
  14.4 1.4 %shard_map.56 = (bf16[512,1024]{1,0:T(8,128)(2,1)S(1)}, bf16[512,256]{1,0:T(8,128)(2,1)S(1)}, bf16[1024,256]{1,0:T(8,128)(2,1)S(1)}) custom-call(s32[1,512]{1,0:T(1,128)S(1)} %get-tuple-element.16.freq_ref, bf16[256,1024]{1,0:T(8,128)(2,1)S(1)} %get-tuple-element.17.velocity_ref, f32[1024,256]{1,0:T(8,128)S(1)} %get-tuple-element.18.matrix_ref), custom_call_target="tpu_custom_call" | custom-call | flops 1 | bytes 1 | tf_op jit(solution)/shard_map/pallas_call | solution.py:142
  16.5 0.0 collective-permute-done.spectra_ref
  16.5 0.0 all-to-all-done.basis_ref
  16.5 3.8 %collective-permute-start.1 = (bf16[4,256,256]{2,1,0:T(8,128)(2,1)S(1)}, bf16[4,256,256]{2,1,0:T(8,128)(2,1)S(1)}, u32[]{:S(2)}, u32[]{:S(2)}) collective-permute-start(bf16[4,256,256]{2,1,0:T(8,128)(2,1)S(1)} %all-to-all-done.basis_ref), channel_id=1, source_target_pairs={{0,4},{4,0},{1,5},{5,1},{2,6},{6,2},{3,7},{7,3},{8,12},{12,8},{9,1... | collective-permute-start | bytes 1572872 | tf_op jit(solution)/shard_map/ppermute | solution.py:273
  20.3 0.4 shard_map.57.before_ref
  20.8 1.1 collective-permute-done.1.basis_ref
  21.8 0.4 shard_map.58
  22.3 18.7 %all_to_all.30.parts_ref = bf16[16,128,256]{2,1,0:T(8,128)(2,1)S(1)} all-to-all(bf16[16,128,256]{2,1,0:T(8,128)(2,1)S(1)} %bitcast.14), channel_id=1, replica_groups=mesh['band_0'=16,'band_1'=4,'band_2'=2,'mode'=4] {'mode','band_1'}, dimensions={0} | all-to-all | bytes 2097152 | tf_op jit(solution)/shard_map/all_to_all | solution.py:269
  41.0 0.1 shard_map.59
  41.1 25.3 %all_to_all.31.parts_ref = bf16[16,8,256]{2,1,0:T(8,128)(2,1)S(1)} all-to-all(bf16[16,8,256]{2,1,0:T(8,128)(2,1)S(1)} %bitcast.15), channel_id=1, replica_groups=mesh['band_0'=16,'band_1'=4,'band_2'=2,'mode'=4] {'band_0'}, dimensions={0} | all-to-all | bytes 131072 | tf_op jit(solution)/shard_map/all_to_all | solution.py:269
  66.4 6.6 %all_to_all.32.coef_ref = bf16[4,8,256]{2,1,0:T(8,128)(2,1)S(1)} all-to-all(bf16[4,8,256]{2,1,0:T(8,128)(2,1)S(1)} %shard_map.60), channel_id=1, replica_groups=mesh['band_0'=16,'band_1'=4,'band_2'=2,'mode'=4] {'mode'}, dimensions={0} | all-to-all | bytes 32768 | tf_op jit(solution)/shard_map/all_to_all | solution.py:269
  73.0 0.2 shard_map.61
  73.1 14.3 %all_to_all.33 = bf16[16,8,256]{2,1,0:T(8,128)(2,1)S(1)} all-to-all(bf16[16,8,256]{2,1,0:T(8,128)(2,1)S(1)} %shard_map.61), channel_id=1, replica_groups=mesh['band_0'=16,'band_1'=4,'band_2'=2,'mode'=4] {'band_0'}, dimensions={0} | all-to-all | bytes 131072 | tf_op jit(solution)/shard_map/all_to_all | solution.py:269
  87.4 0.1 broadcast_in_dim.10
  87.5 14.9 %all_to_all.34 = bf16[16,128,256]{2,1,0:T(8,128)(2,1)S(1)} all-to-all(bf16[16,128,256]{2,1,0:T(8,128)(2,1)S(1)} %broadcast_in_dim.10), channel_id=1, replica_groups=mesh['band_0'=16,'band_1'=4,'band_2'=2,'mode'=4] {'mode','band_1'}, dimensions={0} | all-to-all | bytes 2097152 | tf_op jit(solution)/shard_map/all_to_all | solution.py:269
  102.5 0.8 shard_map.63
  103.3 9.0 %collective-permute-start.2 = (bf16[256,1024]{1,0:T(8,128)(2,1)S(1)}, bf16[256,1024]{1,0:T(8,128)(2,1)S(1)}, u32[]{:S(2)}, u32[]{:S(2)}) collective-permute-start(bf16[256,1024]{1,0:T(8,128)(2,1)S(1)} %shard_map.63), channel_id=1, source_target_pairs={{0,4},{4,0},{1,5},{5,1},{2,6},{6,2},{3,7},{7,3},{8,12},{12,8},{9,1... | collective-permute-start | bytes 1572872 | tf_op jit(solution)/shard_map/ppermute | solution.py:273
  112.3 0.8 shard_map.62
  113.1 0.7 collective-permute-done.2
  113.8 0.9 fusion
  (2 shorter events, 0.0 us)
Async XLA Ops:
  0.0 16.5 %all-to-all-start = ((bf16[4,256,256]{2,1,0:T(8,128)(2,1)}), bf16[4,256,256]{2,1,0:T(8,128)(2,1)S(1)}, u32[]{:S(2)}, u32[]{:S(2)}) async-start(bf16[4,256,256]{2,1,0:T(8,128)(2,1)} %bitcast.18), calls=%async_computation | async-start | bytes 1048576 | tf_op jit(solution)/shard_map/all_to_all | solution.py:269
  7.0 9.5 %collective-permute-start = (bf16[512,256]{1,0:T(8,128)(2,1)S(1)}, bf16[512,256]{1,0:T(8,128)(2,1)S(1)}, u32[]{:S(2)}, u32[]{:S(2)}) collective-permute-start(bf16[512,256]{1,0:T(8,128)(2,1)S(1)} %get-tuple-element.20), channel_id=1, source_target_pairs={{0,4},{4,0},{1,5},{5,1},{2,6},{6,2},{3,7},{7,3},{8,12},{12,8},{9,1... | collective-permute-start | bytes 786440 | tf_op jit(solution)/shard_map/ppermute | solution.py:273
  16.5 5.3 %collective-permute-start.1 = (bf16[4,256,256]{2,1,0:T(8,128)(2,1)S(1)}, bf16[4,256,256]{2,1,0:T(8,128)(2,1)S(1)}, u32[]{:S(2)}, u32[]{:S(2)}) collective-permute-start(bf16[4,256,256]{2,1,0:T(8,128)(2,1)S(1)} %all-to-all-done.basis_ref), channel_id=1, source_target_pairs={{0,4},{4,0},{1,5},{5,1},{2,6},{6,2},{3,7},{7,3},{8,12},{12,8},{9,1... | collective-permute-start | bytes 1572872 | tf_op jit(solution)/shard_map/ppermute | solution.py:273
  103.3 10.5 %collective-permute-start.2 = (bf16[256,1024]{1,0:T(8,128)(2,1)S(1)}, bf16[256,1024]{1,0:T(8,128)(2,1)S(1)}, u32[]{:S(2)}, u32[]{:S(2)}) collective-permute-start(bf16[256,1024]{1,0:T(8,128)(2,1)S(1)} %shard_map.63), channel_id=1, source_target_pairs={{0,4},{4,0},{1,5},{5,1},{2,6},{6,2},{3,7},{7,3},{8,12},{12,8},{9,1... | collective-permute-start | bytes 1572872 | tf_op jit(solution)/shard_map/ppermute | solution.py:273

commit v7 on v4

--- a/solution.py
+++ b/solution.py
@@ -242,9 +242,9 @@
 
 def history_kernel(basis_ref, forcing_ref, table_ref, *rest):
     out_ref = rest[-1]
-    total = dot_t(basis_ref[0], forcing_ref[0])
-    for k in range(1, basis_ref.shape[0]):
-        total = total + dot_t(basis_ref[k], forcing_ref[k])
+    blocks = range(basis_ref.shape[0])
+    basis = jnp.concatenate([basis_ref[k] for k in blocks], axis=1)
+    total = dot_t(basis, jnp.concatenate([forcing_ref[k] for k in blocks], axis=1))
     out_ref[...] = dot(total.astype(BF16), table_ref[...]).astype(out_ref.dtype)
 
 

time: 115 us -> 115 us (level)
  no operation moved by 1% of the time
where the time goes in v7:
time: 115 us
  blocking collectives  79.7 us (69%)
  starting transfers between devices  25.1 us (22%)
  Pallas kernels  6.42 us (6%)
  waiting for transfers between devices  1.77 us (2%)
    all_to_all x5, blocking collectives, exchange(): return lax.all_to_all(value, axis, split_axis=0, concat_axis=0, tiled=True)  79.7 us
    ppermute x3, starting transfers between devices, swap_cores(): return lax.ppermute(value, CORE, [(0, 1), (1, 0)])  20.2 us
    all_to_all x1, starting transfers between devices, exchange(): return lax.all_to_all(value, axis, split_axis=0, concat_axis=0, tiled=True)  4.84 us
  transfers between devices with their start and end apart: 4, of which 2 were waited for; matrix products, arithmetic and copies ran while one was open for 0% of the time, Pallas kernels for 4%

profile of v7, /device:TPU:1, one launch (start us, length us, event | category | flops | bytes accessed | tf_op | source)
XLA Modules:
  0.0 114.7 jit_solution(9544312696115750638)
XLA Ops:
  0.0 4.8 %all-to-all-start = ((bf16[4,256,256]{2,1,0:T(8,128)(2,1)}), bf16[4,256,256]{2,1,0:T(8,128)(2,1)S(1)}, u32[]{:S(2)}, u32[]{:S(2)}) async-start(bf16[4,256,256]{2,1,0:T(8,128)(2,1)} %bitcast.19), calls=%async_computation | async-start | bytes 1048576 | tf_op jit(solution)/shard_map/all_to_all | solution.py:270
  4.8 2.2 %shard_map.55 = (bf16[512,256]{1,0:T(8,128)(2,1)S(1)}, s32[1,512]{1,0:T(1,128)S(1)}, bf16[256,1024]{1,0:T(8,128)(2,1)S(1)}, f32[1024,256]{1,0:T(8,128)S(1)}) custom-call(s32[1]{0:T(128)} %bitcast.1.place_ref, s32[1,512]{1,0:T(1,128)} %bitcast.21, bf16[256,1024]{1,0:T(8,128)(2,1)} %bitcast.18, f32[1024,256]{1,0:T(8,128)} %bitcast.17), custom_call_target="tpu_custom_call" | custom-call | flops 1 | bytes 1 | tf_op jit(solution)/shard_map/pallas_call | solution.py:129
  7.0 7.4 %collective-permute-start = (bf16[512,256]{1,0:T(8,128)(2,1)S(1)}, bf16[512,256]{1,0:T(8,128)(2,1)S(1)}, u32[]{:S(2)}, u32[]{:S(2)}) collective-permute-start(bf16[512,256]{1,0:T(8,128)(2,1)S(1)} %get-tuple-element.20), channel_id=1, source_target_pairs={{0,4},{4,0},{1,5},{5,1},{2,6},{6,2},{3,7},{7,3},{8,12},{12,8},{9,1... | collective-permute-start | bytes 786440 | tf_op jit(solution)/shard_map/ppermute | solution.py:274
  14.5 1.4 %shard_map.56 = (bf16[512,1024]{1,0:T(8,128)(2,1)S(1)}, bf16[512,256]{1,0:T(8,128)(2,1)S(1)}, bf16[1024,256]{1,0:T(8,128)(2,1)S(1)}) custom-call(s32[1]{0:T(128)} %bitcast.1.place_ref, s32[1,512]{1,0:T(1,128)S(1)} %get-tuple-element.16.freq_ref, bf16[256,1024]{1,0:T(8,128)(2,1)S(1)} %get-tuple-element.17.velocity_ref, ...), custom_call_target="tpu_custom_call" | custom-call | flops 1 | bytes 1 | tf_op jit(solution)/shard_map/pallas_call | solution.py:143
  16.5 0.0 collective-permute-done.spectra_ref
  16.5 0.0 all-to-all-done.basis_ref
  16.5 3.8 %collective-permute-start.1 = (bf16[4,256,256]{2,1,0:T(8,128)(2,1)S(1)}, bf16[4,256,256]{2,1,0:T(8,128)(2,1)S(1)}, u32[]{:S(2)}, u32[]{:S(2)}) collective-permute-start(bf16[4,256,256]{2,1,0:T(8,128)(2,1)S(1)} %all-to-all-done.basis_ref), channel_id=1, source_target_pairs={{0,4},{4,0},{1,5},{5,1},{2,6},{6,2},{3,7},{7,3},{8,12},{12,8},{9,1... | collective-permute-start | bytes 1572872 | tf_op jit(solution)/shard_map/ppermute | solution.py:274
  20.3 0.4 shard_map.57.before_ref
  20.8 1.1 collective-permute-done.1.basis_ref
  21.8 0.4 shard_map.58
  22.3 18.7 %all_to_all.30.parts_ref = bf16[16,128,256]{2,1,0:T(8,128)(2,1)S(1)} all-to-all(bf16[16,128,256]{2,1,0:T(8,128)(2,1)S(1)} %bitcast.15), channel_id=1, replica_groups=mesh['band_0'=16,'band_1'=4,'band_2'=2,'mode'=4] {'mode','band_1'}, dimensions={0} | all-to-all | bytes 2097152 | tf_op jit(solution)/shard_map/all_to_all | solution.py:270
  40.9 0.1 shard_map.59
  41.1 25.3 %all_to_all.31.parts_ref = bf16[16,8,256]{2,1,0:T(8,128)(2,1)S(1)} all-to-all(bf16[16,8,256]{2,1,0:T(8,128)(2,1)S(1)} %bitcast.16), channel_id=1, replica_groups=mesh['band_0'=16,'band_1'=4,'band_2'=2,'mode'=4] {'band_0'}, dimensions={0} | all-to-all | bytes 131072 | tf_op jit(solution)/shard_map/all_to_all | solution.py:270
  66.4 6.6 %all_to_all.32.coef_ref = bf16[4,8,256]{2,1,0:T(8,128)(2,1)S(1)} all-to-all(bf16[4,8,256]{2,1,0:T(8,128)(2,1)S(1)} %shard_map.60), channel_id=1, replica_groups=mesh['band_0'=16,'band_1'=4,'band_2'=2,'mode'=4] {'mode'}, dimensions={0} | all-to-all | bytes 32768 | tf_op jit(solution)/shard_map/all_to_all | solution.py:270
  73.0 0.2 shard_map.61
  73.1 14.3 %all_to_all.33 = bf16[16,8,256]{2,1,0:T(8,128)(2,1)S(1)} all-to-all(bf16[16,8,256]{2,1,0:T(8,128)(2,1)S(1)} %shard_map.61), channel_id=1, replica_groups=mesh['band_0'=16,'band_1'=4,'band_2'=2,'mode'=4] {'band_0'}, dimensions={0} | all-to-all | bytes 131072 | tf_op jit(solution)/shard_map/all_to_all | solution.py:270
  87.4 0.1 broadcast_in_dim.10
  87.5 14.9 %all_to_all.34 = bf16[16,128,256]{2,1,0:T(8,128)(2,1)S(1)} all-to-all(bf16[16,128,256]{2,1,0:T(8,128)(2,1)S(1)} %broadcast_in_dim.10), channel_id=1, replica_groups=mesh['band_0'=16,'band_1'=4,'band_2'=2,'mode'=4] {'mode','band_1'}, dimensions={0} | all-to-all | bytes 2097152 | tf_op jit(solution)/shard_map/all_to_all | solution.py:270
  102.5 0.8 shard_map.63
  103.3 9.0 %collective-permute-start.2 = (bf16[256,1024]{1,0:T(8,128)(2,1)S(1)}, bf16[256,1024]{1,0:T(8,128)(2,1)S(1)}, u32[]{:S(2)}, u32[]{:S(2)}) collective-permute-start(bf16[256,1024]{1,0:T(8,128)(2,1)S(1)} %shard_map.63), channel_id=1, source_target_pairs={{0,4},{4,0},{1,5},{5,1},{2,6},{6,2},{3,7},{7,3},{8,12},{12,8},{9,1... | collective-permute-start | bytes 1572872 | tf_op jit(solution)/shard_map/ppermute | solution.py:274
  112.3 0.8 shard_map.62
  113.1 0.7 collective-permute-done.2
  113.8 0.9 fusion
  (2 shorter events, 0.0 us)
Async XLA Ops:
  0.0 16.5 %all-to-all-start = ((bf16[4,256,256]{2,1,0:T(8,128)(2,1)}), bf16[4,256,256]{2,1,0:T(8,128)(2,1)S(1)}, u32[]{:S(2)}, u32[]{:S(2)}) async-start(bf16[4,256,256]{2,1,0:T(8,128)(2,1)} %bitcast.19), calls=%async_computation | async-start | bytes 1048576 | tf_op jit(solution)/shard_map/all_to_all | solution.py:270
  7.0 9.5 %collective-permute-start = (bf16[512,256]{1,0:T(8,128)(2,1)S(1)}, bf16[512,256]{1,0:T(8,128)(2,1)S(1)}, u32[]{:S(2)}, u32[]{:S(2)}) collective-permute-start(bf16[512,256]{1,0:T(8,128)(2,1)S(1)} %get-tuple-element.20), channel_id=1, source_target_pairs={{0,4},{4,0},{1,5},{5,1},{2,6},{6,2},{3,7},{7,3},{8,12},{12,8},{9,1... | collective-permute-start | bytes 786440 | tf_op jit(solution)/shard_map/ppermute | solution.py:274
  16.5 5.3 %collective-permute-start.1 = (bf16[4,256,256]{2,1,0:T(8,128)(2,1)S(1)}, bf16[4,256,256]{2,1,0:T(8,128)(2,1)S(1)}, u32[]{:S(2)}, u32[]{:S(2)}) collective-permute-start(bf16[4,256,256]{2,1,0:T(8,128)(2,1)S(1)} %all-to-all-done.basis_ref), channel_id=1, source_target_pairs={{0,4},{4,0},{1,5},{5,1},{2,6},{6,2},{3,7},{7,3},{8,12},{12,8},{9,1... | collective-permute-start | bytes 1572872 | tf_op jit(solution)/shard_map/ppermute | solution.py:274
  103.3 10.5 %collective-permute-start.2 = (bf16[256,1024]{1,0:T(8,128)(2,1)S(1)}, bf16[256,1024]{1,0:T(8,128)(2,1)S(1)}, u32[]{:S(2)}, u32[]{:S(2)}) collective-permute-start(bf16[256,1024]{1,0:T(8,128)(2,1)S(1)} %shard_map.63), channel_id=1, source_target_pairs={{0,4},{4,0},{1,5},{5,1},{2,6},{6,2},{3,7},{7,3},{8,12},{12,8},{9,1... | collective-permute-start | bytes 1572872 | tf_op jit(solution)/shard_map/ppermute | solution.py:274
